TPU v7x, 128 devices: a whole 4x4x4 slice. The times are simulated.
128 devices in a mesh: dom: 32 (over y, x, core), grid: 4 (over z).
Axes of the slice: x: 4, y: 4, z: 4, core: 2. Of those that a mesh axis runs over, the one named last changes fastest.
Arguments:
- charges: float32 [131072], P(('dom', 'grid')), may hold values from -4 to 4
- fractions: float32 [3, 131072], P(None, ('dom', 'grid')), may hold values from 0 to 1
- bases: int32 [3, 131072], P(None, ('dom', 'grid')), may hold values from 0 to 255, as said below
- counts: int32 [128], P(('dom', 'grid')), may hold values from 256 to 1024, as said below
Outputs:
- forces: float32 [3, 131072], P(None, ('dom', 'grid'))
Inputs may be any that keep to these rules, and one draw needn't show every extreme that they name: Slot r belongs to device p = r // 1024 of dom+grid; with c = p // 16 (0 .. 7) and e = p % 16, bases[0, r] lies in c * 32 .. c * 32 + 31 and bases[1, r] in e * 16 .. e * 16 + 15. `counts`: some domain is full in every draw.
All inputs are finite; a program needn't handle non-finite values.
Results may differ from a plain program's by a relative error of at most 0.0003.
Values sent between devices are 32-bit elements; how exact they have to be, the bound alone decides.
A program may use at most 64 MiB of HBM per device.

v0:
```python
import math

import jax
import jax.numpy as jnp
from jax import lax
from jax.sharding import PartitionSpec as P

G = 256
DOMX = 8


ewald_beta = 0.6
field_scale = 1.0
highest = lax.Precision.HIGHEST


def spline_table(fraction):
    remainder = 1.0 - fraction
    square = fraction * fraction
    cubic_term = square * fraction
    values = jnp.stack(
        [
            remainder * remainder * remainder / 6.0,
            (3.0 * cubic_term - 6.0 * square + 4.0) / 6.0,
            (-3.0 * cubic_term + 3.0 * square + 3.0 * fraction + 1.0) / 6.0,
            cubic_term / 6.0,
        ]
    )
    slopes = jnp.stack(
        [
            -0.5 * remainder * remainder,
            0.5 * (3.0 * square - 4.0 * fraction),
            0.5 * (-3.0 * square + 2.0 * fraction + 1.0),
            0.5 * square,
        ]
    )
    return (values, slopes)


def signed_wave(number, length):
    return jnp.where(number < length // 2, number, number - length).astype(jnp.float32)


def bspline_modulus(number, length):
    phase_angle = number.astype(jnp.float32) * (2.0 * math.pi / length)
    return 9.0 / (2.0 + jnp.cos(phase_angle)) ** 2


def influence(wave_first, wave_second, wave_third, length, strength):
    squared = (
        signed_wave(wave_first, length) ** 2
        + signed_wave(wave_second, length) ** 2
        + signed_wave(wave_third, length) ** 2
    )
    positive = squared > 0.0
    guarded = jnp.where(positive, squared, 1.0)
    damping = jnp.exp(-((math.pi / (ewald_beta * length)) ** 2) * squared)
    moduli = (
        bspline_modulus(wave_first, length)
        * bspline_modulus(wave_second, length)
        * bspline_modulus(wave_third, length)
    )
    return jnp.where(positive, strength * moduli * damping / guarded, 0.0)


def site_gradient(
    sampled, values_first, slopes_first, values_second, slopes_second, values_third, slopes_third
):
    along_third = jnp.sum(sampled * values_third[None, None], axis=2)
    slope_third = jnp.sum(sampled * slopes_third[None, None], axis=2)
    grad_first = jnp.sum(jnp.sum(along_third * values_second[None], axis=1) * slopes_first, axis=0)
    grad_second = jnp.sum(jnp.sum(along_third * slopes_second[None], axis=1) * values_first, axis=0)
    grad_third = jnp.sum(jnp.sum(slope_third * values_second[None], axis=1) * values_first, axis=0)
    return jnp.stack([grad_first, grad_second, grad_third])


def dft_tables(length):
    numbers = jnp.arange(length, dtype=jnp.int32)
    product = numbers[:, None] * numbers[None, :] % length
    phase_angle = product.astype(jnp.float32) * (2.0 * math.pi / length)
    return (jnp.cos(phase_angle), jnp.sin(phase_angle))


def fold_matrix(domain_count, span, padded, length):
    column = jnp.arange(domain_count * padded, dtype=jnp.int32)
    target = (column // padded * span + column % padded) % length
    cells = jnp.arange(length, dtype=jnp.int32)
    return (cells[:, None] == target[None, :]).astype(jnp.float32)


def send_charges(blocks):
    return lax.all_to_all(blocks, ("dom", "grid"), split_axis=0, concat_axis=1, tiled=True)


def return_potential(outgoing):
    return lax.all_to_all(outgoing, ("dom", "grid"), split_axis=1, concat_axis=0, tiled=True)


def assemble(arrived, components, rows_first, rows_second, domains_second, fold_first, fold_second):
    depth = arrived.shape[0]
    pieces = arrived.reshape(
        depth, DOMX, domains_second, components, rows_first, rows_second
    ).transpose(3, 0, 1, 4, 2, 5)
    pieces = pieces.reshape(components, depth, DOMX * rows_first, domains_second * rows_second)
    partial_rows = jnp.einsum("csab,yb->csay", pieces, fold_second, precision=highest)
    return jnp.einsum("csay,xa->csxy", partial_rows, fold_first, precision=highest)


def scatter_pieces(fields, domains_second, padded_first, padded_second, fold_first, fold_second):
    components = fields.shape[0]
    depth = fields.shape[1]
    strip = jnp.einsum("csxy,yb->csxb", fields, fold_second, precision=highest)
    pieces_out = jnp.einsum("csxb,xa->csab", strip, fold_first, precision=highest)
    pieces_out = pieces_out.reshape(
        components, depth, DOMX, padded_first, domains_second, padded_second
    ).transpose(1, 2, 4, 0, 3, 5)
    return pieces_out.reshape(
        depth, DOMX * domains_second, components * padded_first * padded_second
    )


def planes_potential(plane_real, plane_imag, position, cosine, sine, length, strength):
    depth = plane_real.shape[0]
    row_real = jnp.einsum("sxy,yk->sxk", plane_real, cosine, precision=highest) + jnp.einsum(
        "sxy,yk->sxk", plane_imag, sine, precision=highest
    )
    row_imag = jnp.einsum("sxy,yk->sxk", plane_imag, cosine, precision=highest) - jnp.einsum(
        "sxy,yk->sxk", plane_real, sine, precision=highest
    )
    full_real = jnp.einsum("kx,sxy->sky", cosine, row_real, precision=highest) + jnp.einsum(
        "kx,sxy->sky", sine, row_imag, precision=highest
    )
    full_imag = jnp.einsum("kx,sxy->sky", cosine, row_imag, precision=highest) - jnp.einsum(
        "kx,sxy->sky", sine, row_real, precision=highest
    )
    numbers = jnp.arange(length, dtype=jnp.int32)
    wave_third = position * depth + jnp.arange(depth, dtype=jnp.int32)[:, None, None]
    factor = influence(numbers[None, :, None], numbers[None, None, :], wave_third, length, strength)
    full_real = full_real * factor
    full_imag = full_imag * factor
    back_real = jnp.einsum("xk,sky->sxy", cosine, full_real, precision=highest) - jnp.einsum(
        "xk,sky->sxy", sine, full_imag, precision=highest
    )
    back_imag = jnp.einsum("xk,sky->sxy", cosine, full_imag, precision=highest) + jnp.einsum(
        "xk,sky->sxy", sine, full_real, precision=highest
    )
    out_real = jnp.einsum("sxk,ky->sxy", back_real, cosine, precision=highest) - jnp.einsum(
        "sxk,ky->sxy", back_imag, sine, precision=highest
    )
    out_imag = jnp.einsum("sxk,ky->sxy", back_imag, cosine, precision=highest) + jnp.einsum(
        "sxk,ky->sxy", back_real, sine, precision=highest
    )
    return (out_real, out_imag)


def local(charges, fractions, bases, counts):
    device_count = lax.axis_size(("dom", "grid"))
    position = lax.axis_index(("dom", "grid"))
    domains_second = device_count // DOMX
    span_first = G // DOMX
    span_second = G // domains_second
    padded_first = span_first + 3
    padded_second = span_second + 3
    block_first = position // domains_second
    block_second = position % domains_second
    atom_count = charges.shape[0]
    alive_rows = (jnp.arange(atom_count, dtype=jnp.int32) < counts[0]).astype(jnp.float32)
    weighted = charges * alive_rows
    values_first, slopes_first = spline_table(fractions[0])
    values_second, slopes_second = spline_table(fractions[1])
    values_third, slopes_third = spline_table(fractions[2])
    offsets = jnp.arange(4, dtype=jnp.int32)
    local_first = bases[0] - block_first * span_first
    local_second = bases[1] - block_second * span_second
    flat_index = (
        (bases[2][None, None, None, :] + offsets[None, None, :, None])
        % G
        * (padded_first * padded_second)
        + (local_first[None, None, None, :] + offsets[:, None, None, None]) * padded_second
        + (local_second[None, None, None, :] + offsets[None, :, None, None])
    )
    shares = (
        weighted
        * values_first[:, None, None, :]
        * values_second[None, :, None, :]
        * values_third[None, None, :, :]
    )
    block = (
        jnp.zeros((G * padded_first * padded_second,), jnp.float32)
        .at[flat_index.reshape(-1)]
        .add(shares.reshape(-1))
    )
    block = block.reshape(G, padded_first, padded_second)
    fold_first = fold_matrix(DOMX, span_first, padded_first, G)
    fold_second = fold_matrix(domains_second, span_second, padded_second, G)
    rows_first = block.shape[1]
    rows_second = block.shape[2]
    cell_count = rows_first * rows_second
    cosine, sine = dft_tables(G)
    strength = field_scale * G**3.5 / math.sqrt(atom_count * device_count)
    flat_columns = block.reshape(G, cell_count)
    column_real = jnp.dot(cosine, flat_columns, precision=highest)
    column_imag = -jnp.dot(sine, flat_columns, precision=highest)
    outgoing_planes = jnp.concatenate([column_real, column_imag], axis=1).reshape(
        G, 1, 2 * cell_count
    )
    arrived = send_charges(outgoing_planes)
    planes = assemble(arrived, 2, rows_first, rows_second, domains_second, fold_first, fold_second)
    field_real, field_imag = planes_potential(
        planes[0], planes[1], position, cosine, sine, G, strength
    )
    outgoing = scatter_pieces(
        jnp.stack([field_real, field_imag]),
        domains_second,
        padded_first,
        padded_second,
        fold_first,
        fold_second,
    )
    returned = return_potential(outgoing)
    spectral = returned.reshape(G, 2, padded_first * padded_second)
    potential_block = (
        jnp.dot(cosine, spectral[:, 0], precision=highest)
        - jnp.dot(sine, spectral[:, 1], precision=highest)
    ) / float(G**3)
    sampled = potential_block.reshape(-1)[flat_index]
    gradient = site_gradient(
        sampled,
        values_first,
        slopes_first,
        values_second,
        slopes_second,
        values_third,
        slopes_third,
    )
    return -weighted[None, :] * gradient


def solution(mesh):
    placed = (
        P(("dom", "grid")),
        P(None, ("dom", "grid")),
        P(None, ("dom", "grid")),
        P(("dom", "grid")),
    )
    return jax.shard_map(
        local, mesh=mesh, in_specs=placed, out_specs=P(None, ("dom", "grid")), check_vma=False
    )
```

profile of v0, /device:TPU:1, one launch (start us, length us, event | category | flops | bytes accessed | tf_op | source)
XLA Modules:
  0.0 871.7 jit_solution(1464353423876895080)
XLA Ops:
  0.0 1.5 multiply_multiply_fusion.2
  1.5 0.8 multiply_multiply_fusion.1
  3.0 1.3 fusion.198
  5.0 0.8 fusion.201
  6.7 341.5 %scatter_custom_fusion = f32[170240]{0:T(1024)S(1)} fusion(s32[65536]{0:T(1024)S(1)} %bitcast.145, f32[65536]{0:T(1024)S(1)} %bitcast.144, f32[]{:T(128)} %constant.147.clone.1), kind=kCustom, calls=%fused_computation.47 | custom fusion | flops 65536 | bytes 680964 | tf_op jit(solution)/shard_map/scatter-add | solution.py:191
  348.2 0.7 reshape_reshape.3
  348.9 2.2 convolution_negate_fusion
  351.1 2.2 fusion.74
  353.4 3.1 copy.65
  356.5 11.5 %all-to-all-start = ((f32[256,1,1330]{2,1,0:T(1,128)}), f32[256,1,1330]{2,1,0:T(1,128)S(1)}, u32[]{:S(2)}, u32[]{:S(2)}) async-start(f32[256,1,1330]{2,1,0:T(1,128)} %copy.65), calls=%async_computation | async-start | bytes 2883584 | tf_op jit(solution)/shard_map/all_to_all | solution.py:92
  368.9 0.8 broadcast_multiply_fusion
  369.7 21.8 %all-to-all-done = f32[256,1,1330]{2,1,0:T(1,128)S(1)} async-done(((f32[256,1,1330]{2,1,0:T(1,128)}), f32[256,1,1330]{2,1,0:T(1,128)S(1)}, u32[]{:S(2)}, u32[]{:S(2)}) %all-to-all-start) | async-done | bytes 1361952 | tf_op jit(solution)/shard_map/all_to_all | solution.py:92
  391.7 7.4 reshape.457
  399.1 9.4 %copy.67 = f32[2,2,8,35,16,19]{3,2,5,4,1,0:T(8,128)} copy(f32[2,2,8,35,16,19]{5,3,0,4,2,1:T(8,128)} %bitcast.137) | data formatting | bytes 2723840 | tf_op jit(solution)/shard_map/transpose | solution.py:103
  408.4 4.1 reshape.458
  412.5 1.9 fusion.26
  414.5 1.2 convolution_bitcast_fusion.1
  415.7 1.6 fusion.20
  417.2 1.6 fusion.21
  418.8 1.6 convolution_add_fusion.3
  420.4 1.8 fusion.53
  422.2 1.6 convolution_subtract_fusion.4
  423.7 2.0 fusion.48
  425.8 2.0 fusion.8
  427.8 1.6 fusion.50
  429.3 2.0 fusion.6
  431.3 1.6 fusion.44
  432.9 1.6 fusion.4
  434.5 2.2 fusion.46
  436.7 1.6 fusion.3
  438.3 1.8 fusion.42
  440.1 1.9 fusion.2
  442.0 1.9 fusion.1
  443.8 0.8 fusion.9
  444.6 2.2 convolution_bitcast_fusion
  446.8 1.9 copy.77
  448.7 3.3 reshape.459
  452.0 9.1 %copy.94 = f32[2,8,16,2,35,19]{5,4,3,0,2,1:T(8,128)} copy(f32[2,8,16,2,35,19]{4,1,5,2,0,3:T(8,128)} %bitcast.138) | data formatting | bytes 2723840 | tf_op jit(solution)/shard_map/reshape | solution.py:117
  461.1 9.2 %reshape.484 = f32[2,128,1330]{2,0,1:T(2,128)} reshape(f32[2,8,16,2,35,19]{5,4,3,0,2,1:T(8,128)} %copy.94) | data formatting | bytes 2723840 | tf_op jit(solution)/shard_map/reshape | solution.py:117
  470.3 3.9 all-to-all-start.1
  474.3 23.6 %all-to-all-done.1 = f32[2,128,1330]{2,0,1:T(2,128)S(1)} async-done(((f32[2,128,1330]{2,0,1:T(2,128)}), f32[2,128,1330]{2,0,1:T(2,128)S(1)}, u32[]{:S(2)}, u32[]{:S(2)}) %all-to-all-start.1) | async-done | bytes 1361952 | tf_op jit(solution)/shard_map/all_to_all | solution.py:96
  497.8 2.2 reshape.461
  500.0 1.2 fusion.200
  501.2 0.9 copy.80
  502.1 1.7 fusion.14
  503.9 0.9 copy.81
  504.8 1.7 fusion
  507.4 362.7 %gather_fusion = f32[65536]{0:T(1024)S(1)} fusion(f32[170240]{0:T(1024)S(1)} %reshape.462, s32[65536]{0:T(1024)S(1)} %broadcast_clamp_fusion), kind=kCustom, calls=%fused_computation | custom fusion | bytes 786432 | tf_op jit(solution)/shard_map/gather | solution.py:226
  (66 shorter events, 4.6 us)
Async XLA Ops:
  1.5 4.4 copy-start.5
  1.5 4.4 copy-start.7
  1.5 4.4 copy-start.9
  1.5 4.4 copy-start.11
  4.4 0.6 copy-start.1
  356.5 35.1 %all-to-all-start = ((f32[256,1,1330]{2,1,0:T(1,128)}), f32[256,1,1330]{2,1,0:T(1,128)S(1)}, u32[]{:S(2)}, u32[]{:S(2)}) async-start(f32[256,1,1330]{2,1,0:T(1,128)} %copy.65), calls=%async_computation | async-start | bytes 2883584 | tf_op jit(solution)/shard_map/all_to_all | solution.py:92
  422.2 3.6 copy-start
  470.3 27.5 %all-to-all-start.1 = ((f32[2,128,1330]{2,0,1:T(2,128)}), f32[2,128,1330]{2,0,1:T(2,128)S(1)}, u32[]{:S(2)}, u32[]{:S(2)}) async-start(f32[2,128,1330]{2,0,1:T(2,128)} %reshape.484), calls=%async_computation.1 | async-start | bytes 2883584 | tf_op jit(solution)/shard_map/all_to_all | solution.py:96
  507.3 362.9 %copy-start.2 = (f32[4,1024]{1,0:T(4,128)S(1)}, f32[4,1024]{1,0:T(4,128)}, u32[]{:S(2)}) copy-start(f32[4,1024]{1,0:T(4,128)} %copy-done.1) | copy-start | bytes 49156
  507.3 362.9 %copy-start.4 = (f32[4,1024]{1,0:T(4,128)S(1)}, f32[4,1024]{1,0:T(4,128)}, u32[]{:S(2)}) copy-start(f32[4,1024]{1,0:T(4,128)} %get-tuple-element.48) | copy-start | bytes 49156
  507.3 363.3 %copy-start.3 = (f32[4,1024]{1,0:T(4,128)S(1)}, f32[4,1024]{1,0:T(4,128)}, u32[]{:S(2)}) copy-start(f32[4,1024]{1,0:T(4,128)} %get-tuple-element.47) | copy-start | bytes 49156
  507.3 363.4 %copy-start.6 = (f32[1,1024]{1,0:T(1,128)S(1)}, f32[1,1024]{1,0:T(1,128)}, u32[]{:S(2)}) copy-start(f32[1,1024]{1,0:T(1,128)} %copy-done.5) | copy-start | bytes 12292
  507.3 363.4 %copy-start.8 = (f32[1,1024]{1,0:T(1,128)S(1)}, f32[1,1024]{1,0:T(1,128)}, u32[]{:S(2)}) copy-start(f32[1,1024]{1,0:T(1,128)} %copy-done.7) | copy-start | bytes 12292
  507.3 363.4 %copy-start.10 = (f32[1,1024]{1,0:T(1,128)S(1)}, f32[1,1024]{1,0:T(1,128)}, u32[]{:S(2)}) copy-start(f32[1,1024]{1,0:T(1,128)} %copy-done.9) | copy-start | bytes 12292
  507.3 363.4 %copy-start.12 = (f32[1,1024]{1,0:T(1,128)S(1)}, f32[1,1024]{1,0:T(1,128)}, u32[]{:S(2)}) copy-start(f32[1,1024]{1,0:T(1,128)} %copy-done.11) | copy-start | bytes 12292
  507.4 363.5 %copy-start.13 = (f32[1,1024]{1,0:T(1,128)S(1)}, f32[1,1024]{1,0:T(1,128)}, u32[]{:S(2)}) copy-start(f32[1,1024]{1,0:T(1,128)} %get-tuple-element.16) | copy-start | bytes 12292
  507.4 363.5 %copy-start.14 = (f32[1,1024]{1,0:T(1,128)S(1)}, f32[1,1024]{1,0:T(1,128)}, u32[]{:S(2)}) copy-start(f32[1,1024]{1,0:T(1,128)} %get-tuple-element.20) | copy-start | bytes 12292
  507.4 363.5 %copy-start.15 = (f32[1,1024]{1,0:T(1,128)S(1)}, f32[1,1024]{1,0:T(1,128)}, u32[]{:S(2)}) copy-start(f32[1,1024]{1,0:T(1,128)} %get-tuple-element.21) | copy-start | bytes 12292
  507.4 363.5 %copy-start.16 = (f32[1,1024]{1,0:T(1,128)S(1)}, f32[1,1024]{1,0:T(1,128)}, u32[]{:S(2)}) copy-start(f32[1,1024]{1,0:T(1,128)} %get-tuple-element.22) | copy-start | bytes 12292
  507.4 363.5 %copy-start.17 = (f32[1024]{0:T(1024)S(1)}, f32[1024]{0:T(1024)}, u32[]{:S(2)}) copy-start(f32[1024]{0:T(1024)} %get-tuple-element.12) | copy-start | bytes 12292
where the time goes:
time: 880 us; the launch traced here: 872 us
  local copies, waits for them, and re-layouts  418 us (48%)
  other arithmetic  349 us (40%)
  waiting for transfers between devices  45.4 us (5%)
  matrix products  41.9 us (5%)
  starting transfers between devices  15.4 us (2%)
    gather x2, local copies, waits for them, and re-layouts, local(): sampled = potential_block.reshape(-1)[flat_index]  363 us
    scatter-add x1, other arithmetic, local(): block = jnp.zeros((G * padded_first * padded_second,), jnp.float32).at[fl...  342 us
    all_to_all x1, waiting for transfers between devices, return_potential(): lax.all_to_all(outgoing, ('dom', 'grid'), split_axis=1, concat_axis=0, ti...  23.6 us
    all_to_all x1, waiting for transfers between devices, send_charges(): lax.all_to_all(blocks, ('dom', 'grid'), split_axis=0, concat_axis=1, tile...  21.8 us
    reshape x2, local copies, waits for them, and re-layouts, scatter_pieces(): pieces_out.reshape(depth, DOMX * domains_second, components * padded_firs...  18.3 us
  transfers between devices with their start and end apart: 2, of which 2 were waited for; matrix products, arithmetic and copies ran while one was open for 0% of the time, Pallas kernels for 0%

commit v1 on v0

v1 whole, which is shorter than its diff:
```python
import functools
import math

import jax
import jax.numpy as jnp
import numpy as np
import ml_dtypes
from jax import lax
from jax.experimental import pallas as pl
from jax.experimental.pallas import tpu as pltpu
from jax.sharding import PartitionSpec as P

G = 256
DOMX, DOMY = 8, 16
SPANX, SPANY = 32, 16
PADX, PADY = 40, 19
N = DOMX * DOMY
ATOM_DEV = 1024
LANES = 768
TILES = LANES // 128
ROWS = 2 * TILES
REPS = 72
HALF = G
ewald_beta = 0.6
field_scale = 1.0
MESH = pl.DeviceIdType.MESH
f32, bf16 = jnp.float32, jnp.bfloat16


def halves(table):
    high = table.astype(ml_dtypes.bfloat16)
    low = (table - high.astype(np.float64)).astype(ml_dtypes.bfloat16)
    return high, low


def lane_cells():
    lane = np.arange(LANES)
    y, x = lane // PADX, lane % PADX
    valid = (x < SPANX + 3) & (y < PADY)
    return x, y, valid


def self_and_pairs(first, second):
    selfs, pairs, seen = [], [], set()
    for a in range(first):
        for b in range(second):
            if (a, b) in seen:
                continue
            mirror = ((-a) % first, (-b) % second)
            seen.update([(a, b), mirror])
            (selfs if mirror == (a, b) else pairs).append((a, b))
    return selfs, pairs


def modulus(k):
    return 9.0 / (2.0 + np.cos(2.0 * np.pi * k / G)) ** 2


def signed(k):
    return np.where(k < G // 2, k, k - G).astype(np.float64)


def tables():
    out = {}
    wave = np.arange(G // 2)
    grid = np.arange(G)
    turn = 2.0 * np.pi / G
    first = np.cos(turn * (wave[:, None] * grid[None, :] % G))
    second = np.sin(turn * (wave[:, None] * grid[None, :] % G))
    second[0] = np.cos(np.pi * grid)
    out["basis"] = np.concatenate([first, second])

    x, y, valid = lane_cells()
    selfs, pairs = self_and_pairs(DOMX, DOMY)
    reps = pairs + selfs
    weight = np.array([2.0] * len(pairs) + [1.0] * len(selfs))
    kap = np.array([a for a, b in reps])
    lam = np.array([b for a, b in reps])
    source = np.arange(N)
    c, e = source // DOMY, source % DOMY
    steps = (2 * kap[:, None] * c[None, :] + lam[:, None] * e[None, :]) % 16
    angle = 2.0 * np.pi / 16 * steps
    left = np.zeros((2, 2, REPS, 2, N))
    for j in range(2):
        left[0, j, : len(reps), j] = np.cos(angle)
        left[1, j, : len(reps), j] = np.where(steps % 8 == 0, 0.0, -np.sin(angle))
    left = left.reshape(4 * REPS, 2 * N)
    out["left"], out["left_back"] = left, left.T

    phase = turn * ((kap[:, None] * x[None, :] + lam[:, None] * y[None, :]) % G)
    twiddle = np.zeros((2, REPS, LANES))
    twiddle[0, : len(reps)] = np.cos(phase) * valid
    twiddle[1, : len(reps)] = np.sin(phase) * valid
    out["twiddle"] = twiddle

    selfs_in, pairs_in = self_and_pairs(SPANX, SPANY)
    plus = pairs_in + selfs_in[:2]
    minus = [((-a) % SPANX, (-b) % SPANY) for a, b in pairs_in] + selfs_in[2:]

    def inner(modes):
        m = np.array([a for a, b in modes])
        n = np.array([b for a, b in modes])
        return 2.0 * np.pi / 32 * ((x[:, None] * m[None, :] + 2 * y[:, None] * n[None, :]) % 32)

    right = np.concatenate(
        [
            np.cos(inner(plus)),
            np.sin(inner(pairs_in)),
            np.cos(inner(selfs_in[2:])),
        ],
        axis=1,
    )
    out["right"] = right * valid[:, None]

    rate = (np.pi / (ewald_beta * G)) ** 2
    bump = np.zeros((4, REPS, HALF))
    bump[2:] = 1.0
    for row, modes in enumerate((plus, minus)):
        kx = kap[:, None] + DOMX * np.array([a for a, b in modes])[None, :]
        ky = lam[:, None] + DOMY * np.array([b for a, b in modes])[None, :]
        square = signed(kx) ** 2 + signed(ky) ** 2
        bump[row, : len(reps)] = weight[:, None] * modulus(kx) * modulus(ky) * np.exp(-rate * square)
        bump[2 + row, : len(reps)] = square
    out["bump"] = bump

    strength = field_scale * G**3.5 / math.sqrt(N * ATOM_DEV)
    along = np.zeros((N, 128))
    for j in range(2):
        k = wave.copy()
        share = np.full(N, 2.0)
        share[0] = 1.0
        if j == 1:
            k[0] = G // 2
        square = signed(k) ** 2
        along[:, j] = strength * modulus(k) * np.exp(-rate * square) * share / float(G) ** 3
        along[:, 2 + j] = square
    out["along"] = along
    return out


def split(value):
    high = value.astype(bf16)
    return high, (value - high.astype(f32)).astype(bf16)


def dot3(a, b, dims=((1,), (0,))):
    def one(p, q):
        return lax.dot_general(p, q, (dims, ((), ())), preferred_element_type=f32)

    return one(a[0], b[0]) + (one(a[0], b[1]) + one(a[1], b[0]))


def splines(u):
    rest = 1.0 - u
    square = u * u
    cube = square * u
    values = [
        rest * rest * rest / 6.0,
        (3.0 * cube - 6.0 * square + 4.0) / 6.0,
        (-3.0 * cube + 3.0 * square + 3.0 * u + 1.0) / 6.0,
        cube / 6.0,
    ]
    slopes = [
        -0.5 * rest * rest,
        0.5 * (3.0 * square - 4.0 * u),
        0.5 * (-3.0 * square + 2.0 * u + 1.0),
        0.5 * square,
    ]
    return values, slopes


def spread(rows, first, terms, wrap=None):
    shape = (rows, first.shape[1])
    offset = lax.broadcasted_iota(jnp.int32, shape, 0) - first
    if wrap:
        offset = offset & (wrap - 1)
    masks = [offset == a for a in range(4)]
    outs = []
    for term in terms:
        total = jnp.where(masks[3], term[3], 0.0)
        for a in (2, 1, 0):
            total = jnp.where(masks[a], term[a], total)
        outs.append(total)
    return outs


def body(
    charges, fractions, bases, counts, basis, left, left_back, right, twiddle, bump, along,
    out, tw, bt, send, recv, back, home, gt, sems, own,
):
    p = lax.axis_index("dom") * 4 + lax.axis_index("grid")
    barrier = pltpu.get_barrier_semaphore()

    def peer(i):
        d = lax.rem(p + i, N)
        return d, (d // 4, lax.rem(d, 4))

    def greet(i, carry):
        pl.semaphore_signal(barrier, inc=1, device_id=peer(i)[1], device_id_type=MESH)
        return carry

    lax.fori_loop(1, N, greet, 0)

    def exchange(source, target, which):
        def go(i, carry):
            d, where = peer(i)
            pltpu.make_async_remote_copy(
                src_ref=source.at[d], dst_ref=target.at[p], send_sem=sems.at[2 * which],
                recv_sem=sems.at[2 * which + 1], device_id=where, device_id_type=MESH,
            ).start()
            return carry

        lax.fori_loop(1, N, go, 0)
        mine = pltpu.make_async_copy(source.at[p], target.at[p], own)
        mine.start()
        mine.wait()
        every = pltpu.make_async_remote_copy(
            src_ref=source.at[pl.ds(0, N - 1)], dst_ref=target.at[pl.ds(0, N - 1)],
            send_sem=sems.at[2 * which], recv_sem=sems.at[2 * which + 1],
            device_id=peer(1)[1], device_id_type=MESH,
        )
        every.wait_send()
        every.wait_recv()

    values, slopes = splines(fractions[...])
    alive = lax.broadcasted_iota(jnp.int32, (1, ATOM_DEV), 1) < counts[0]
    weighted = jnp.where(alive, charges[...], 0.0)

    def row(which, terms):
        return [t[which : which + 1] for t in terms]

    wz, sz = spread(G, bases[2:3], (row(2, values), row(2, slopes)), G)
    base = (basis[0], basis[1])
    for part, table in enumerate((wz, sz)):
        high, low = split(dot3(base, split(table)))
        tw[0, part] = high
        tw[1, part] = low

    local_x = bases[0:1] - (p // DOMY) * SPANX
    local_y = bases[1:2] - lax.rem(p, DOMY) * SPANY
    wx, sx = spread(PADX, local_x, (row(0, values), row(0, slopes)))
    wy, sy = spread(24, local_y, (row(1, values), row(1, slopes)))
    charged = wx * weighted
    for y in range(0, PADY, 2):
        pieces = [charged * wy[y : y + 1]]
        if y + 1 < PADY:
            pieces.append(charged * wy[y + 1 : y + 2])
        else:
            pieces.append(jnp.zeros((8, ATOM_DEV), f32))
        piece = jnp.concatenate(pieces, axis=0)
        high, low = split(piece)
        bt[0, pl.ds(y * PADX, piece.shape[0])] = high
        bt[1, pl.ds(y * PADX, piece.shape[0])] = low

    planes = dot3((tw[0, 0], tw[1, 0]), (bt[0], bt[1]), ((1,), (1,)))
    for j in range(2):
        for t in range(TILES):
            send[:, j * TILES + t, :] = planes[j * N : (j + 1) * N, t * 128 : (t + 1) * 128]

    pl.semaphore_wait(barrier, N - 1)
    exchange(send, recv, 0)

    def gathered(buffer):
        parts = [
            jnp.concatenate([buffer[:, j * TILES + t, :] for t in range(TILES)], axis=1)
            for j in range(2)
        ]
        return jnp.concatenate(parts, axis=0)

    first = dot3((left[0], left[1]), split(gathered(recv)))
    real, imag = first[: 2 * REPS], first[2 * REPS :]
    tc = jnp.concatenate([twiddle[0]] * 2, axis=0)
    ts = jnp.concatenate([twiddle[1]] * 2, axis=0)
    turned = jnp.concatenate([real * tc + imag * ts, imag * tc - real * ts], axis=0)
    wide = (right[0], right[1])
    modes = dot3(split(turned), wide)

    mine = along[pl.ds(p, 1), :]
    lane = lax.broadcasted_iota(jnp.int32, (REPS, HALF), 1)
    paired = lane < HALF - 2
    ones, twos, cross = [], [], []
    for j in range(2):
        scale, square = mine[:, j : j + 1], mine[:, 2 + j : 3 + j]
        both = []
        for side in range(2):
            whole = bump[2 + side] + square
            positive = whole > 0.0
            both.append(
                jnp.where(positive, bump[side] * scale / jnp.where(positive, whole, 1.0), 0.0)
            )
        total = both[0] + both[1]
        ones.append(jnp.where(paired, total, both[0]))
        twos.append(jnp.where(paired, total, both[1]))
        cross.append(jnp.where(paired, both[0] - both[1], 0.0))
    f1, f2, fd = (jnp.concatenate(parts, axis=0) for parts in (ones, twos, cross))
    rc, rs = modes[: 2 * REPS, :HALF], modes[: 2 * REPS, HALF:]
    ic, is_ = modes[2 * REPS :, :HALF], modes[2 * REPS :, HALF:]
    filtered = jnp.concatenate(
        [
            jnp.concatenate([f1 * rc + fd * is_, f2 * rs - fd * ic], axis=1),
            jnp.concatenate([f1 * ic - fd * rs, fd * rc + f2 * is_], axis=1),
        ],
        axis=0,
    )
    cells = dot3(split(filtered), wide, ((1,), (1,)))
    real, imag = cells[: 2 * REPS], cells[2 * REPS :]
    turned = jnp.concatenate([real * tc - imag * ts, imag * tc + real * ts], axis=0)
    planes = dot3((left_back[0], left_back[1]), split(turned))
    for j in range(2):
        for t in range(TILES):
            back[:, j * TILES + t, :] = planes[j * N : (j + 1) * N, t * 128 : (t + 1) * 128]
    exchange(back, home, 1)

    high, low = split(gathered(home).T)
    gt[0] = high
    gt[1] = low
    chunk = 256
    for r in range(0, ATOM_DEV, chunk):
        here = slice(r, r + chunk)
        field = dot3((gt[0], gt[1]), (tw[0, 0, :, here], tw[1, 0, :, here]))
        slope = dot3((gt[0], gt[1]), (tw[0, 1, :, here], tw[1, 1, :, here]))
        sums = [jnp.zeros((8, chunk), f32) for _ in range(3)]

        def fold(part):
            return sum(part[8 * i : 8 * i + 8] for i in range(1, PADX // 8)) + part[:8]

        for y in range(PADY):
            here_y = slice(y * PADX, (y + 1) * PADX)
            sums[0] += fold(field[here_y] * sx[:, here]) * wy[y : y + 1, here]
            sums[1] += fold(field[here_y] * wx[:, here]) * sy[y : y + 1, here]
            sums[2] += fold(slope[here_y] * wx[:, here]) * wy[y : y + 1, here]
        for a in range(3):
            total = jnp.sum(sums[a], axis=0, keepdims=True)
            out[a : a + 1, here] = -weighted[:, here] * total


def solution(mesh):
    table = tables()
    pairs = {k: np.stack(halves(table[k])) for k in ("basis", "left", "left_back", "right")}
    plain = {k: table[k].astype(np.float32) for k in ("twiddle", "bump", "along")}
    vmem = pl.BlockSpec(memory_space=pltpu.VMEM)
    smem = pl.BlockSpec(memory_space=pltpu.SMEM)
    call = pl.pallas_call(
        body,
        out_shape=jax.ShapeDtypeStruct((3, ATOM_DEV), f32),
        in_specs=[vmem, vmem, vmem, smem] + [vmem] * 7,
        out_specs=vmem,
        scratch_shapes=[
            pltpu.VMEM((2, 2, G, ATOM_DEV), bf16),
            pltpu.VMEM((2, LANES, ATOM_DEV), bf16),
            pltpu.VMEM((N, ROWS, 128), f32),
            pltpu.VMEM((N, ROWS, 128), f32),
            pltpu.VMEM((N, ROWS, 128), f32),
            pltpu.VMEM((N, ROWS, 128), f32),
            pltpu.VMEM((2, LANES, G), bf16),
            pltpu.SemaphoreType.DMA((4,)),
            pltpu.SemaphoreType.DMA,
        ],
        compiler_params=pltpu.CompilerParams(
            collective_id=1, has_side_effects=True, vmem_limit_bytes=56 << 20
        ),
    )

    def local(charges, fractions, bases, counts):
        return call(
            charges.reshape(1, ATOM_DEV), fractions, bases, counts,
            pairs["basis"], pairs["left"], pairs["left_back"], pairs["right"],
            plain["twiddle"], plain["bump"], plain["along"],
        )

    placed = (
        P(("dom", "grid")),
        P(None, ("dom", "grid")),
        P(None, ("dom", "grid")),
        P(("dom", "grid")),
    )
    return jax.shard_map(
        local, mesh=mesh, in_specs=placed, out_specs=P(None, ("dom", "grid")), check_vma=False
    )
```

time: 880 us -> 50.2 us (0.06)
  local copies, waits for them, and re-layouts: 418 us -> 1.33 us
  other arithmetic: 349 us -> 0 us
  Pallas kernels: 0 us -> 48 us
  waiting for transfers between devices: 45.4 us -> 0 us
  matrix products: 41.9 us -> 0 us
  starting transfers between devices: 15.4 us -> 0 us
    gather x2 -> x0, local copies, waits for them, and re-layouts: 363 us -> none  [local(): sampled = potential_block.reshape(-1)[flat_index]]
    scatter-add x1 -> x0, other arithmetic: 342 us -> none  [local(): block = jnp.zeros((G * padded_first * padded_second,), jnp.float32).at[fl...]
    pallas_call x0 -> x1, Pallas kernels: none -> 48 us  [local(): call(charges.reshape(1, ATOM_DEV), fractions, bases, counts, pairs['basis...]
    all_to_all x2 -> x0, waiting for transfers between devices: 45.4 us -> none  [the longest x1 23.6 us: return_potential(): lax.all_to_all(outgoing, ('dom', 'grid'), split_axis=1, concat_axis=0, ti...]
    dot_general x24 -> x0, matrix products: 41.9 us -> none  [the longest x1 2.23 us: planes_potential(): jnp.einsum('sxk,ky->sxy', back_real, cosine, precision=highest)]
    reshape x8 -> x0, local copies, waits for them, and re-layouts: 38.9 us -> none  [the longest x2 18.3 us: scatter_pieces(): pieces_out.reshape(depth, DOMX * domains_second, components * padded_firs...]
    all_to_all x2 -> x0, starting transfers between devices: 15.4 us -> none  [the longest x1 11.5 us: send_charges(): lax.all_to_all(blocks, ('dom', 'grid'), split_axis=0, concat_axis=1, tile...]
    transpose x2 -> x0, local copies, waits for them, and re-layouts: 11.2 us -> none  [the longest x1 9.36 us: assemble(): pieces = arrived.reshape(depth, DOMX, domains_second, components, rows_fi...]
  transfers between devices with their start and end apart: 2 -> 0, of which waited for: 2 -> 0; matrix products, arithmetic and copies ran while one was open for 0% -> 0% of each run, Pallas kernels for 0% -> 0%
where the time goes in v1:
time: 50.2 us; the launch traced here: 50 us
  Pallas kernels  48 us (96%)
  local copies, waits for them, and re-layouts  1.33 us (3%)
  between operations  0.66 us (1%)
    pallas_call x1, Pallas kernels, local(): call(charges.reshape(1, ATOM_DEV), fractions, bases, counts, pairs['basis...  48 us
    unnamed x1, local copies, waits for them, and re-layouts  1.33 us

profile of v1, /device:TPU:1, one launch (start us, length us, event | category | flops | bytes accessed | tf_op | source)
XLA Modules:
  0.0 50.0 jit_solution(14535745760550688250)
XLA Ops:
  0.7 48.0 %shard_map.109 = f32[3,1024]{1,0:T(4,128)} custom-call(f32[1,1024]{1,0:T(1,128)} %bitcast.1, f32[3,1024]{1,0:T(4,128)} %fractions.1, s32[3,1024]{1,0:T(4,128)} %bases.1, s32[1]{0:T(128)S(6)} %copy.13.counts, bf16[2,256,256]{2,1,0:T(8,128)(2,1)} %constant.14.clone.basis, bf16[2,288,256]{2,1,0:T(8,128)(2,1)} %constant.15.clone.left, ...), custom_call_target="tpu_custom_call" | custom-call | tf_op jit(solution)/shard_map/pallas_call | solution.py:365
  48.7 1.3 %copy.14 = f32[3,1024]{1,0:T(4,128)} copy(f32[3,1024]{1,0:T(4,128)} %shard_map.109) | data formatting | bytes 24576

commit v2 on v1

v2 whole, which is shorter than its diff:
```python
import functools
import math

import jax
import jax.numpy as jnp
import numpy as np
import ml_dtypes
from jax import lax
from jax.experimental import pallas as pl
from jax.experimental.pallas import tpu as pltpu
from jax.sharding import PartitionSpec as P

G = 256
DOMX, DOMY = 8, 16
SPANX, SPANY = 32, 16
PADY = 19
MAIN = PADY * SPANX
RIM = 24
N = DOMX * DOMY
ATOM_DEV = 1024
LANES = 768
HALFTILE = 640
CELLS = 704
TILES = LANES // 128
REPS = 72
HALF = G
ewald_beta = 0.6
field_scale = 1.0
MESH = pl.DeviceIdType.MESH
f32, bf16 = jnp.float32, jnp.bfloat16


def halves(table):
    high = table.astype(ml_dtypes.bfloat16)
    low = (table - high.astype(np.float64)).astype(ml_dtypes.bfloat16)
    return high, low


def lane_cells():
    lane = np.arange(LANES)
    lane = np.where(lane < CELLS, lane, lane - (CELLS - HALFTILE))
    rim = np.maximum(lane - MAIN, 0)
    x = np.where(lane < MAIN, lane % SPANX, SPANX + rim // RIM)
    y = np.where(lane < MAIN, lane // SPANX, rim % RIM)
    return x, y, (x < SPANX + 3) & (y < PADY)


def self_and_pairs(first, second):
    selfs, pairs, seen = [], [], set()
    for a in range(first):
        for b in range(second):
            if (a, b) in seen:
                continue
            mirror = ((-a) % first, (-b) % second)
            seen.update([(a, b), mirror])
            (selfs if mirror == (a, b) else pairs).append((a, b))
    return selfs, pairs


def modulus(k):
    return 9.0 / (2.0 + np.cos(2.0 * np.pi * k / G)) ** 2


def signed(k):
    return np.where(k < G // 2, k, k - G).astype(np.float64)


def tables():
    out = {}
    wave = np.arange(G // 2)
    grid = np.arange(G)
    turn = 2.0 * np.pi / G
    first = np.cos(turn * (wave[:, None] * grid[None, :] % G))
    second = np.sin(turn * (wave[:, None] * grid[None, :] % G))
    second[0] = np.cos(np.pi * grid)
    out["basis"] = np.concatenate([first, second])

    x, y, valid = lane_cells()
    selfs, pairs = self_and_pairs(DOMX, DOMY)
    reps = pairs + selfs
    weight = np.array([2.0] * len(pairs) + [1.0] * len(selfs))
    kap = np.array([a for a, b in reps])
    lam = np.array([b for a, b in reps])
    source = np.arange(N)
    c, e = source // DOMY, source % DOMY
    steps = (2 * kap[:, None] * c[None, :] + lam[:, None] * e[None, :]) % 16
    angle = 2.0 * np.pi / 16 * steps
    left = np.zeros((2, REPS, N))
    left[0, : len(reps)] = np.cos(angle)
    left[1, : len(reps)] = np.where(steps % 8 == 0, 0.0, -np.sin(angle))
    left = left.reshape(2 * REPS, N)
    out["left"], out["left_back"] = left, left.T

    phase = turn * ((kap[:, None] * x[None, :] + lam[:, None] * y[None, :]) % G)
    lane = np.arange(LANES)
    twiddle = np.zeros((2, 2, REPS, LANES))
    for j, kept in enumerate((lane < CELLS, (lane < HALFTILE) | (lane >= CELLS))):
        twiddle[j, 0, : len(reps)] = np.cos(phase) * (valid & kept)
        twiddle[j, 1, : len(reps)] = np.sin(phase) * (valid & kept)
    out["twiddle"] = twiddle

    selfs_in, pairs_in = self_and_pairs(SPANX, SPANY)
    plus = pairs_in + selfs_in[:2]
    minus = [((-a) % SPANX, (-b) % SPANY) for a, b in pairs_in] + selfs_in[2:]

    def inner(modes):
        m = np.array([a for a, b in modes])
        n = np.array([b for a, b in modes])
        return 2.0 * np.pi / 32 * ((x[:, None] * m[None, :] + 2 * y[:, None] * n[None, :]) % 32)

    right = np.concatenate(
        [
            np.cos(inner(plus)),
            np.sin(inner(pairs_in)),
            np.cos(inner(selfs_in[2:])),
        ],
        axis=1,
    )
    out["right"] = right * valid[:, None]

    rate = (np.pi / (ewald_beta * G)) ** 2
    bump = np.zeros((4, REPS, HALF))
    bump[2:] = 1.0
    for row, modes in enumerate((plus, minus)):
        kx = kap[:, None] + DOMX * np.array([a for a, b in modes])[None, :]
        ky = lam[:, None] + DOMY * np.array([b for a, b in modes])[None, :]
        square = signed(kx) ** 2 + signed(ky) ** 2
        bump[row, : len(reps)] = weight[:, None] * modulus(kx) * modulus(ky) * np.exp(-rate * square)
        bump[2 + row, : len(reps)] = square
    out["bump"] = bump

    strength = field_scale * G**3.5 / math.sqrt(N * ATOM_DEV)
    along = np.zeros((N, 128))
    for j in range(2):
        k = wave.copy()
        share = np.full(N, 2.0)
        share[0] = 1.0
        if j == 1:
            k[0] = G // 2
        square = signed(k) ** 2
        along[:, j] = strength * modulus(k) * np.exp(-rate * square) * share / float(G) ** 3
        along[:, 2 + j] = square
    out["along"] = along
    return out


def split(value):
    high = value.astype(bf16)
    return high, (value - high.astype(f32)).astype(bf16)


def dot3(a, b, dims=((1,), (0,))):
    def one(p, q):
        return lax.dot_general(p, q, (dims, ((), ())), preferred_element_type=f32)

    return one(a[0], b[0]) + (one(a[0], b[1]) + one(a[1], b[0]))


def splines(u):
    rest = 1.0 - u
    square = u * u
    cube = square * u
    values = [
        rest * rest * rest / 6.0,
        (3.0 * cube - 6.0 * square + 4.0) / 6.0,
        (-3.0 * cube + 3.0 * square + 3.0 * u + 1.0) / 6.0,
        cube / 6.0,
    ]
    slopes = [
        -0.5 * rest * rest,
        0.5 * (3.0 * square - 4.0 * u),
        0.5 * (-3.0 * square + 2.0 * u + 1.0),
        0.5 * square,
    ]
    return values, slopes


def spread(rows, first, terms, wrap=None):
    shape = (rows, first.shape[1])
    offset = lax.broadcasted_iota(jnp.int32, shape, 0) - first
    if wrap:
        offset = offset & (wrap - 1)
    masks = [offset == a for a in range(4)]
    outs = []
    for term in terms:
        total = jnp.where(masks[3], term[3], 0.0)
        for a in (2, 1, 0):
            total = jnp.where(masks[a], term[a], total)
        outs.append(total)
    return outs


def body(
    charges, fractions, bases, counts, basis_any, left_any, back_any, right_any, twiddle_any, bump_any,
    along, out, basis, left, left_back, right, twiddle, bump, tw, bt, send_a, send_b, recv_a, recv_b,
    back_a, back_b, home_a, home_b, gt, sems, loads,
):
    p = lax.axis_index("dom") * 4 + lax.axis_index("grid")
    barrier = pltpu.get_barrier_semaphore()
    loading = [
        pltpu.make_async_copy(source, target, loads.at[k])
        for k, (source, target) in enumerate(
            (
                (basis_any, basis), (left_any, left), (right_any, right), (twiddle_any, twiddle),
                (bump_any, bump), (back_any, left_back),
            )
        )
    ]
    for load in loading:
        load.start()

    def peer(i):
        d = lax.rem(p + i, N)
        return d, (d // 4, lax.rem(d, 4))

    def greet(i, carry):
        pl.semaphore_signal(barrier, inc=1, device_id=peer(i)[1], device_id_type=MESH)
        return carry

    lax.fori_loop(1, N, greet, 0, unroll=8)

    def post(source, target, which):
        def go(i, carry):
            d, where = peer(i)
            pltpu.make_async_remote_copy(
                src_ref=source.at[d], dst_ref=target.at[p], send_sem=sems.at[2 * which],
                recv_sem=sems.at[2 * which + 1], device_id=where, device_id_type=MESH,
            ).start()
            return carry

        lax.fori_loop(1, N, go, 0, unroll=8)
        target[pl.ds(p, 1)] = source[pl.ds(p, 1)]

    def every(source, target, which):
        return pltpu.make_async_remote_copy(
            src_ref=source.at[pl.ds(0, N - 1)], dst_ref=target.at[pl.ds(0, N - 1)],
            send_sem=sems.at[2 * which], recv_sem=sems.at[2 * which + 1],
            device_id=peer(1)[1], device_id_type=MESH,
        )

    values, slopes = splines(fractions[...])
    alive = lax.broadcasted_iota(jnp.int32, (1, ATOM_DEV), 1) < counts[0]
    weighted = jnp.where(alive, charges[...], 0.0)

    def row(which, terms):
        return [t[which : which + 1] for t in terms]

    (wz,) = spread(G, bases[2:3], (row(2, values),), G)
    wz = split(wz)
    loading[0].wait()
    high, low = split(dot3((basis[0], basis[1]), wz))
    tw[0, 0] = high
    tw[1, 0] = low

    local_x = bases[0:1] - (p // DOMY) * SPANX
    local_y = bases[1:2] - lax.rem(p, DOMY) * SPANY
    wx, sx = spread(40, local_x, (row(0, values), row(0, slopes)))
    wy, sy = spread(RIM, local_y, (row(1, values), row(1, slopes)))
    charged = wx * weighted
    for y in range(PADY):
        high, low = split(charged[:SPANX] * wy[y : y + 1])
        bt[0, pl.ds(y * SPANX, SPANX)] = high
        bt[1, pl.ds(y * SPANX, SPANX)] = low
    rim = [charged[SPANX + a : SPANX + a + 1] * wy for a in range(3)]
    high, low = split(jnp.concatenate(rim + [jnp.zeros((CELLS - MAIN - 3 * RIM, ATOM_DEV), f32)], axis=0))
    for k, part in enumerate((high, low)):
        bt[k, pl.ds(MAIN, CELLS - MAIN)] = part
        bt[k, pl.ds(CELLS, LANES - CELLS)] = part[HALFTILE - MAIN :]

    def to_planes(rows, columns):
        return dot3(
            (tw[0, 0, rows], tw[1, 0, rows]), (bt[0, columns], bt[1, columns]), ((1,), (1,))
        )

    def put(target, value, tiles):
        for t in range(tiles):
            target[:, t, :] = value[:, t * 128 : (t + 1) * 128]

    shared = to_planes(slice(0, G), slice(HALFTILE, LANES))
    side = lax.broadcasted_iota(jnp.int32, (N, 128), 1) < 64
    put(send_a, to_planes(slice(0, N), slice(0, HALFTILE)), TILES - 1)
    send_a[:, TILES - 1, :] = jnp.where(side, shared[:N], shared[N:])
    pl.semaphore_wait(barrier, N - 1)
    post(send_a, recv_a, 0)
    put(send_b, to_planes(slice(N, G), slice(0, HALFTILE)), TILES - 1)
    post(send_b, recv_b, 1)

    for load in loading[1:]:
        load.wait()
    mine = along[pl.ds(p, 1), :]
    lane = lax.broadcasted_iota(jnp.int32, (REPS, HALF), 1)
    paired = lane < HALF - 2
    factors = []
    for j in range(2):
        scale, square = mine[:, j : j + 1], mine[:, 2 + j : 3 + j]
        both = []
        for end in range(2):
            whole = bump[2 + end] + square
            positive = whole > 0.0
            both.append(
                jnp.where(positive, bump[end] * scale / jnp.where(positive, whole, 1.0), 0.0)
            )
        total = both[0] + both[1]
        factors.append(
            (
                jnp.where(paired, total, both[0]),
                jnp.where(paired, total, both[1]),
                jnp.where(paired, both[0] - both[1], 0.0),
            )
        )
    (sz,) = spread(G, bases[2:3], (row(2, slopes),), G)
    high, low = split(dot3((basis[0], basis[1]), split(sz)))
    tw[0, 1] = high
    tw[1, 1] = low

    def filtered(tiles, j):
        high, low = split(jnp.concatenate(tiles, axis=1))
        first = dot3((left[0], left[1]), (high, low))
        real, imag = first[:REPS], first[REPS:]
        tc, ts = twiddle[j, 0], twiddle[j, 1]
        turned = jnp.concatenate([real * tc + imag * ts, imag * tc - real * ts], axis=0)
        wide = (right[0], right[1])
        modes = dot3(split(turned), wide)
        f1, f2, fd = factors[j]
        rc, rs = modes[:REPS, :HALF], modes[:REPS, HALF:]
        ic, is_ = modes[REPS:, :HALF], modes[REPS:, HALF:]
        modes = jnp.concatenate(
            [
                jnp.concatenate([f1 * rc + fd * is_, f2 * rs - fd * ic], axis=1),
                jnp.concatenate([f1 * ic - fd * rs, fd * rc + f2 * is_], axis=1),
            ],
            axis=0,
        )
        cells = dot3(split(modes), wide, ((1,), (1,)))
        real, imag = cells[:REPS], cells[REPS:]
        turned = jnp.concatenate([real * tc - imag * ts, imag * tc + real * ts], axis=0)
        return dot3((left_back[0], left_back[1]), split(turned))

    every(send_a, recv_a, 0).wait_recv()
    plane = filtered([recv_a[:, t, :] for t in range(TILES)], 0)
    put(back_a, plane, TILES - 1)
    back_b[:, TILES - 1, :] = plane[:, HALFTILE:]
    post(back_a, home_a, 2)
    every(send_b, recv_b, 1).wait_recv()
    plane = filtered([recv_b[:, t, :] for t in range(TILES - 1)] + [recv_a[:, TILES - 1, :]], 1)
    put(back_b, plane, TILES - 1)
    back_b[:, TILES - 1, :] += plane[:, HALFTILE:]
    post(back_b, home_b, 3)

    every(send_a, recv_a, 0).wait_send()
    every(send_b, recv_b, 1).wait_send()
    every(back_a, home_a, 2).wait_recv()
    for t in range(TILES - 1):
        high, low = split(home_a[:, t, :].T)
        gt[0, pl.ds(t * 128, 128), :N] = high
        gt[1, pl.ds(t * 128, 128), :N] = low
    every(back_b, home_b, 3).wait_recv()
    for t in range(TILES - 1):
        high, low = split(home_b[:, t, :].T)
        gt[0, pl.ds(t * 128, 128), N:] = high
        gt[1, pl.ds(t * 128, 128), N:] = low
    for k, part in enumerate(split(home_b[:, TILES - 1, :].T)):
        gt[k, HALFTILE:, :N] = part[:64]
        gt[k, HALFTILE:, N:] = part[64:]
    chunk = 256
    for r in range(0, ATOM_DEV, chunk):
        here = slice(r, r + chunk)
        field = dot3((gt[0], gt[1]), (tw[0, 0, :, here], tw[1, 0, :, here]))
        slope = dot3((gt[0], gt[1]), (tw[0, 1, :, here], tw[1, 1, :, here]))
        sums = [jnp.zeros((8, chunk), f32) for _ in range(3)]

        def fold(part):
            return sum(part[8 * i : 8 * i + 8] for i in range(1, part.shape[0] // 8)) + part[:8]

        for y in range(PADY):
            cells = slice(y * SPANX, (y + 1) * SPANX)
            inner = fold(field[cells] * wx[:SPANX, here])
            sums[0] += fold(field[cells] * sx[:SPANX, here]) * wy[y : y + 1, here]
            sums[1] += inner * sy[y : y + 1, here]
            sums[2] += fold(slope[cells] * wx[:SPANX, here]) * wy[y : y + 1, here]
        for a in range(3):
            cells = slice(MAIN + a * RIM, MAIN + (a + 1) * RIM)
            x = slice(SPANX + a, SPANX + a + 1)
            sums[0] += fold(field[cells] * wy[:, here]) * sx[x, here]
            sums[1] += fold(field[cells] * sy[:, here]) * wx[x, here]
            sums[2] += fold(slope[cells] * wy[:, here]) * wx[x, here]
        for a in range(3):
            total = jnp.sum(sums[a], axis=0, keepdims=True)
            out[a : a + 1, here] = -weighted[:, here] * total
    every(back_a, home_a, 2).wait_send()
    every(back_b, home_b, 3).wait_send()


def solution(mesh):
    table = tables()
    pairs = {k: np.stack(halves(table[k])) for k in ("basis", "left", "left_back", "right")}
    plain = {k: table[k].astype(np.float32) for k in ("twiddle", "bump", "along")}
    held = [pairs[k] for k in ("basis", "left", "left_back", "right")]
    held += [plain["twiddle"], plain["bump"]]
    vmem = pl.BlockSpec(memory_space=pltpu.VMEM)
    smem = pl.BlockSpec(memory_space=pltpu.SMEM)
    anywhere = pl.BlockSpec(memory_space=pl.ANY)
    five, six = (pltpu.VMEM((N, rows, 128), f32) for rows in (TILES - 1, TILES))
    call = pl.pallas_call(
        body,
        out_shape=jax.ShapeDtypeStruct((3, ATOM_DEV), f32),
        in_specs=[vmem, vmem, vmem, smem] + [anywhere] * 6 + [vmem],
        out_specs=vmem,
        scratch_shapes=[pltpu.VMEM(a.shape, bf16 if a.dtype != np.float32 else f32) for a in held]
        + [
            pltpu.VMEM((2, 2, G, ATOM_DEV), bf16),
            pltpu.VMEM((2, LANES, ATOM_DEV), bf16),
            six, five, six, five,
            five, six, five, six,
            pltpu.VMEM((2, CELLS, G), bf16),
            pltpu.SemaphoreType.DMA((8,)),
            pltpu.SemaphoreType.DMA((6,)),
        ],
        compiler_params=pltpu.CompilerParams(
            collective_id=1, has_side_effects=True, vmem_limit_bytes=56 << 20
        ),
    )

    def local(charges, fractions, bases, counts):
        return call(
            charges.reshape(1, ATOM_DEV), fractions, bases, counts, *held, plain["along"]
        )

    placed = (
        P(("dom", "grid")),
        P(None, ("dom", "grid")),
        P(None, ("dom", "grid")),
        P(("dom", "grid")),
    )
    return jax.shard_map(
        local, mesh=mesh, in_specs=placed, out_specs=P(None, ("dom", "grid")), check_vma=False
    )
```

time: 50.2 us -> 41.1 us (0.82)
  Pallas kernels: 48 us -> 38.9 us
    pallas_call x1, Pallas kernels: 48 us -> 38.9 us  [local(): call(charges.reshape(1, ATOM_DEV), fractions, bases, counts, *held, plain...]
where the time goes in v2:
time: 41.1 us; the launch traced here: 40.9 us
  Pallas kernels  38.9 us (95%)
  local copies, waits for them, and re-layouts  1.33 us (3%)
  between operations  0.66 us (2%)
    pallas_call x1, Pallas kernels, local(): call(charges.reshape(1, ATOM_DEV), fractions, bases, counts, *held, plain...  38.9 us
    unnamed x1, local copies, waits for them, and re-layouts  1.33 us

profile of v2, /device:TPU:1, one launch (start us, length us, event | category | flops | bytes accessed | tf_op | source)
XLA Modules:
  0.0 40.9 jit_solution(9512558490398712707)
XLA Ops:
  0.7 38.9 %shard_map.109 = f32[3,1024]{1,0:T(4,128)} custom-call(f32[1,1024]{1,0:T(1,128)} %bitcast.1, f32[3,1024]{1,0:T(4,128)} %fractions.1, s32[3,1024]{1,0:T(4,128)} %bases.1, s32[1]{0:T(128)S(6)} %copy.13.counts, bf16[2,256,256]{2,1,0:T(8,128)(2,1)} %constant.14.clone.basis_any, bf16[2,144,128]{2,1,0:T(8,128)(2,1)} %constant.15.clone.left_any, ...), custom_call_target="tpu_custom_call" | custom-call | tf_op jit(solution)/shard_map/pallas_call | solution.py:425
  39.6 1.3 %copy.14 = f32[3,1024]{1,0:T(4,128)} copy(f32[3,1024]{1,0:T(4,128)} %shard_map.109) | data formatting | bytes 24576

commit v3 on v2

--- a/solution.py
+++ b/solution.py
@@ -144,6 +144,14 @@
     return out
 
 
+def far_first():
+    hops = (0, 1, 2, 1)
+    offsets = [(y, x, c, z) for y in range(4) for x in range(4) for c in range(2) for z in range(4)]
+    spread_out = np.random.RandomState(1).permutation(len(offsets))
+    offsets = [offsets[k] for k in spread_out if any(offsets[k])]
+    return sorted(offsets, key=lambda o: -(hops[o[0]] + hops[o[1]] + hops[o[3]]))
+
+
 def split(value):
     high = value.astype(bf16)
     return high, (value - high.astype(f32)).astype(bf16)
@@ -191,53 +199,55 @@
 
 
 def body(
-    charges, fractions, bases, counts, basis_any, left_any, back_any, right_any, twiddle_any, bump_any,
-    along, out, basis, left, left_back, right, twiddle, bump, tw, bt, send_a, send_b, recv_a, recv_b,
-    back_a, back_b, home_a, home_b, gt, sems, loads,
+    charges_any, fractions_any, bases_any, counts, basis_any, left_any, back_any, right_any, twiddle_any,
+    bump_any, along_any, out, basis, left, left_back, right, twiddle, bump, along,
+    charges, fractions, bases, tw, bt, send_a, send_b, recv_a, recv_b,
+    back_a, back_b, home_a, home_b, gt, early, sems, loads,
 ):
-    p = lax.axis_index("dom") * 4 + lax.axis_index("grid")
+    dom, z = lax.axis_index("dom"), lax.axis_index("grid")
+    p = dom * 4 + z
     barrier = pltpu.get_barrier_semaphore()
     loading = [
         pltpu.make_async_copy(source, target, loads.at[k])
         for k, (source, target) in enumerate(
             (
-                (basis_any, basis), (left_any, left), (right_any, right), (twiddle_any, twiddle),
-                (bump_any, bump), (back_any, left_back),
+                (fractions_any, fractions), (bases_any, bases), (charges_any, charges), (basis_any, basis),
+                (left_any, left), (right_any, right), (twiddle_any, twiddle),
+                (bump_any, bump), (along_any, along), (back_any, left_back),
             )
         )
     ]
     for load in loading:
         load.start()
 
-    def peer(i):
-        d = lax.rem(p + i, N)
-        return d, (d // 4, lax.rem(d, 4))
-
-    def greet(i, carry):
-        pl.semaphore_signal(barrier, inc=1, device_id=peer(i)[1], device_id_type=MESH)
-        return carry
-
-    lax.fori_loop(1, N, greet, 0, unroll=8)
+    ys = [lax.rem(dom // 8 + k, 4) * 8 for k in range(4)]
+    xs = [lax.rem(lax.rem(dom, 8) // 2 + k, 4) * 2 for k in range(4)]
+    cores = [lax.rem(dom + k, 2) for k in range(2)]
+    zs = [lax.rem(z + k, 4) for k in range(4)]
+    chips = [[a + b for b in xs] for a in ys]
+    peers = [(chips[a][b] + cores[c], zs[k]) for a, b, c, k in far_first()]
+
+    for where in peers:
+        pl.semaphore_signal(barrier, inc=1, device_id=where, device_id_type=MESH)
 
     def post(source, target, which):
-        def go(i, carry):
-            d, where = peer(i)
+        for where in peers:
             pltpu.make_async_remote_copy(
-                src_ref=source.at[d], dst_ref=target.at[p], send_sem=sems.at[2 * which],
-                recv_sem=sems.at[2 * which + 1], device_id=where, device_id_type=MESH,
+                src_ref=source.at[where[0] * 4 + where[1]], dst_ref=target.at[p],
+                send_sem=sems.at[2 * which], recv_sem=sems.at[2 * which + 1],
+                device_id=where, device_id_type=MESH,
             ).start()
-            return carry
-
-        lax.fori_loop(1, N, go, 0, unroll=8)
         target[pl.ds(p, 1)] = source[pl.ds(p, 1)]
 
     def every(source, target, which):
         return pltpu.make_async_remote_copy(
             src_ref=source.at[pl.ds(0, N - 1)], dst_ref=target.at[pl.ds(0, N - 1)],
             send_sem=sems.at[2 * which], recv_sem=sems.at[2 * which + 1],
-            device_id=peer(1)[1], device_id_type=MESH,
+            device_id=peers[0], device_id_type=MESH,
         )
 
+    for load in loading[:3]:
+        load.wait()
     values, slopes = splines(fractions[...])
     alive = lax.broadcasted_iota(jnp.int32, (1, ATOM_DEV), 1) < counts[0]
     weighted = jnp.where(alive, charges[...], 0.0)
@@ -247,7 +257,7 @@
 
     (wz,) = spread(G, bases[2:3], (row(2, values),), G)
     wz = split(wz)
-    loading[0].wait()
+    loading[3].wait()
     high, low = split(dot3((basis[0], basis[1]), wz))
     tw[0, 0] = high
     tw[1, 0] = low
@@ -265,27 +275,25 @@
     high, low = split(jnp.concatenate(rim + [jnp.zeros((CELLS - MAIN - 3 * RIM, ATOM_DEV), f32)], axis=0))
     for k, part in enumerate((high, low)):
         bt[k, pl.ds(MAIN, CELLS - MAIN)] = part
-        bt[k, pl.ds(CELLS, LANES - CELLS)] = part[HALFTILE - MAIN :]
-
-    def to_planes(rows, columns):
-        return dot3(
-            (tw[0, 0, rows], tw[1, 0, rows]), (bt[0, columns], bt[1, columns]), ((1,), (1,))
-        )
+
+    planes = dot3((bt[0], bt[1]), (tw[0, 0], tw[1, 0]), ((1,), (1,)))
 
     def put(target, value, tiles):
         for t in range(tiles):
             target[:, t, :] = value[:, t * 128 : (t + 1) * 128]
 
-    shared = to_planes(slice(0, G), slice(HALFTILE, LANES))
-    side = lax.broadcasted_iota(jnp.int32, (N, 128), 1) < 64
-    put(send_a, to_planes(slice(0, N), slice(0, HALFTILE)), TILES - 1)
-    send_a[:, TILES - 1, :] = jnp.where(side, shared[:N], shared[N:])
+    def put_turned(target, value):
+        for t in range(TILES - 1):
+            target[:, t, :] = value[t * 128 : (t + 1) * 128].T
+
+    put_turned(send_a, planes[:, :N])
+    send_a[:, TILES - 1, :] = jnp.concatenate([planes[HALFTILE:, :N], planes[HALFTILE:, N:]], axis=0).T
     pl.semaphore_wait(barrier, N - 1)
     post(send_a, recv_a, 0)
-    put(send_b, to_planes(slice(N, G), slice(0, HALFTILE)), TILES - 1)
+    put_turned(send_b, planes[:, N:])
     post(send_b, recv_b, 1)
 
-    for load in loading[1:]:
+    for load in loading[4:]:
         load.wait()
     mine = along[pl.ds(p, 1), :]
     lane = lax.broadcasted_iota(jnp.int32, (REPS, HALF), 1)
@@ -349,29 +357,13 @@
 
     every(send_a, recv_a, 0).wait_send()
     every(send_b, recv_b, 1).wait_send()
-    every(back_a, home_a, 2).wait_recv()
-    for t in range(TILES - 1):
-        high, low = split(home_a[:, t, :].T)
-        gt[0, pl.ds(t * 128, 128), :N] = high
-        gt[1, pl.ds(t * 128, 128), :N] = low
-    every(back_b, home_b, 3).wait_recv()
-    for t in range(TILES - 1):
-        high, low = split(home_b[:, t, :].T)
-        gt[0, pl.ds(t * 128, 128), N:] = high
-        gt[1, pl.ds(t * 128, 128), N:] = low
-    for k, part in enumerate(split(home_b[:, TILES - 1, :].T)):
-        gt[k, HALFTILE:, :N] = part[:64]
-        gt[k, HALFTILE:, N:] = part[64:]
     chunk = 256
-    for r in range(0, ATOM_DEV, chunk):
-        here = slice(r, r + chunk)
-        field = dot3((gt[0], gt[1]), (tw[0, 0, :, here], tw[1, 0, :, here]))
-        slope = dot3((gt[0], gt[1]), (tw[0, 1, :, here], tw[1, 1, :, here]))
+
+    def fold(part):
+        return sum(part[8 * i : 8 * i + 8] for i in range(1, part.shape[0] // 8)) + part[:8]
+
+    def gather(here, field, slope):
         sums = [jnp.zeros((8, chunk), f32) for _ in range(3)]
-
-        def fold(part):
-            return sum(part[8 * i : 8 * i + 8] for i in range(1, part.shape[0] // 8)) + part[:8]
-
         for y in range(PADY):
             cells = slice(y * SPANX, (y + 1) * SPANX)
             inner = fold(field[cells] * wx[:SPANX, here])
@@ -379,13 +371,58 @@
             sums[1] += inner * sy[y : y + 1, here]
             sums[2] += fold(slope[cells] * wx[:SPANX, here]) * wy[y : y + 1, here]
         for a in range(3):
-            cells = slice(MAIN + a * RIM, MAIN + (a + 1) * RIM)
+            cells = slice(MAIN + a * RIM, min(MAIN + (a + 1) * RIM, field.shape[0]))
+            if cells.start >= field.shape[0]:
+                continue
             x = slice(SPANX + a, SPANX + a + 1)
-            sums[0] += fold(field[cells] * wy[:, here]) * sx[x, here]
-            sums[1] += fold(field[cells] * sy[:, here]) * wx[x, here]
-            sums[2] += fold(slope[cells] * wy[:, here]) * wx[x, here]
+            rows = slice(0, cells.stop - cells.start)
+            sums[0] += fold(field[cells] * wy[rows, here]) * sx[x, here]
+            sums[1] += fold(field[cells] * sy[rows, here]) * wx[x, here]
+            sums[2] += fold(slope[cells] * wy[rows, here]) * wx[x, here]
+        return sums
+
+    def gather_tail(sums, here, field, slope):
+        for row in range(HALFTILE, MAIN + 3 * RIM, 8):
+            a, y = (row - MAIN) // RIM, (row - MAIN) % RIM
+            x, rows = slice(SPANX + a, SPANX + a + 1), slice(y, y + 8)
+            cells = slice(row - HALFTILE, row - HALFTILE + 8)
+            sums[0] += field[cells] * wy[rows, here] * sx[x, here]
+            sums[1] += field[cells] * sy[rows, here] * wx[x, here]
+            sums[2] += slope[cells] * wy[rows, here] * wx[x, here]
+
+    def dot(a, b):
+        return jnp.dot(a, b, preferred_element_type=f32)
+
+    def columns(j, part, here):
+        rows = slice(j * N, (j + 1) * N)
+        high = tw[0, part, rows, here]
+        return jnp.concatenate([high, high], axis=0), tw[1, part, rows, here]
+
+    def fields(j, part, here):
+        twice, low = columns(j, part, here)
+        return dot(gt[j, :HALFTILE], twice) + dot(gt[j, :HALFTILE, :N], low)
+
+    def turn(home, j):
+        for t in range(TILES - 1):
+            rows = pl.ds(t * 128, 128)
+            gt[j, rows, :N], gt[j, rows, N:] = split(home[:, t, :].T)
+
+    chunks = [slice(r, r + chunk) for r in range(0, ATOM_DEV, chunk)]
+    every(back_a, home_a, 2).wait_recv()
+    turn(home_a, 0)
+    for here in chunks:
+        for a, part in enumerate(gather(here, fields(0, 0, here), fields(0, 1, here))):
+            early[a, :, here] = part
+    every(back_b, home_b, 3).wait_recv()
+    turn(home_b, 1)
+    shared = home_b[:, TILES - 1, :].T
+    shared = split(jnp.concatenate([shared[:64], shared[64:]], axis=1))
+    for here in chunks:
+        sums = gather(here, fields(1, 0, here), fields(1, 1, here))
+        tails = [dot3(shared, (tw[0, k, :, here], tw[1, k, :, here])) for k in range(2)]
+        gather_tail(sums, here, *tails)
         for a in range(3):
-            total = jnp.sum(sums[a], axis=0, keepdims=True)
+            total = jnp.sum(sums[a] + early[a, :, here], axis=0, keepdims=True)
             out[a : a + 1, here] = -weighted[:, here] * total
     every(back_a, home_a, 2).wait_send()
     every(back_b, home_b, 3).wait_send()
@@ -396,7 +433,7 @@
     pairs = {k: np.stack(halves(table[k])) for k in ("basis", "left", "left_back", "right")}
     plain = {k: table[k].astype(np.float32) for k in ("twiddle", "bump", "along")}
     held = [pairs[k] for k in ("basis", "left", "left_back", "right")]
-    held += [plain["twiddle"], plain["bump"]]
+    held += [plain["twiddle"], plain["bump"], plain["along"]]
     vmem = pl.BlockSpec(memory_space=pltpu.VMEM)
     smem = pl.BlockSpec(memory_space=pltpu.SMEM)
     anywhere = pl.BlockSpec(memory_space=pl.ANY)
@@ -404,17 +441,21 @@
     call = pl.pallas_call(
         body,
         out_shape=jax.ShapeDtypeStruct((3, ATOM_DEV), f32),
-        in_specs=[vmem, vmem, vmem, smem] + [anywhere] * 6 + [vmem],
+        in_specs=[anywhere] * 3 + [smem] + [anywhere] * 7,
         out_specs=vmem,
         scratch_shapes=[pltpu.VMEM(a.shape, bf16 if a.dtype != np.float32 else f32) for a in held]
         + [
+            pltpu.VMEM((1, ATOM_DEV), f32),
+            pltpu.VMEM((3, ATOM_DEV), f32),
+            pltpu.VMEM((3, ATOM_DEV), jnp.int32),
             pltpu.VMEM((2, 2, G, ATOM_DEV), bf16),
-            pltpu.VMEM((2, LANES, ATOM_DEV), bf16),
+            pltpu.VMEM((2, CELLS, ATOM_DEV), bf16),
             six, five, six, five,
             five, six, five, six,
-            pltpu.VMEM((2, CELLS, G), bf16),
+            pltpu.VMEM((2, HALFTILE, G), bf16),
+            pltpu.VMEM((3, 8, ATOM_DEV), f32),
             pltpu.SemaphoreType.DMA((8,)),
-            pltpu.SemaphoreType.DMA((6,)),
+            pltpu.SemaphoreType.DMA((10,)),
         ],
         compiler_params=pltpu.CompilerParams(
             collective_id=1, has_side_effects=True, vmem_limit_bytes=56 << 20
@@ -423,7 +464,7 @@
 
     def local(charges, fractions, bases, counts):
         return call(
-            charges.reshape(1, ATOM_DEV), fractions, bases, counts, *held, plain["along"]
+            charges.reshape(1, ATOM_DEV), fractions, bases, counts, *held
         )
 
     placed = (

time: 41.1 us -> 39.4 us (0.959)
  Pallas kernels: 38.9 us -> 37.2 us
    pallas_call x1, Pallas kernels: 38.9 us -> 37.2 us  [local(): return call(charges.reshape(1, ATOM_DEV), fractions, bases, counts, *held)]
where the time goes in v3:
time: 39.4 us; the launch traced here: 39.2 us
  Pallas kernels  37.2 us (94%)
  local copies, waits for them, and re-layouts  1.33 us (3%)
  between operations  0.66 us (2%)
    pallas_call x1, Pallas kernels, local(): return call(charges.reshape(1, ATOM_DEV), fractions, bases, counts, *held)  37.2 us
    unnamed x1, local copies, waits for them, and re-layouts  1.33 us

profile of v3, /device:TPU:1, one launch (start us, length us, event | category | flops | bytes accessed | tf_op | source)
XLA Modules:
  0.0 39.2 jit_solution(14698366399717874350)
XLA Ops:
  0.7 37.2 %shard_map.109 = f32[3,1024]{1,0:T(4,128)} custom-call(f32[1,1024]{1,0:T(1,128)} %bitcast.1, f32[3,1024]{1,0:T(4,128)} %fractions_any.1, s32[3,1024]{1,0:T(4,128)} %bases_any.1, s32[1]{0:T(128)S(6)} %copy.13.counts, bf16[2,256,256]{2,1,0:T(8,128)(2,1)} %constant.14.clone.basis_any, bf16[2,144,128]{2,1,0:T(8,128)(2,1)} %constant.15.clone.left_any, ...), custom_call_target="tpu_custom_call" | custom-call | tf_op jit(solution)/shard_map/pallas_call | solution.py:466
  37.9 1.3 %copy.14 = f32[3,1024]{1,0:T(4,128)} copy(f32[3,1024]{1,0:T(4,128)} %shard_map.109) | data formatting | bytes 24576

commit v4 on v3

--- a/solution.py
+++ b/solution.py
@@ -22,12 +22,18 @@
 HALFTILE = 640
 CELLS = 704
 TILES = LANES // 128
+SELFS, PAIRS = 4, 62
 REPS = 72
 HALF = G
 ewald_beta = 0.6
 field_scale = 1.0
 MESH = pl.DeviceIdType.MESH
 f32, bf16 = jnp.float32, jnp.bfloat16
+
+
+def side_by_side(table):
+    high, low = halves(table)
+    return np.block([[high, high], [low, np.zeros_like(low)]])
 
 
 def halves(table):
@@ -77,8 +83,8 @@
 
     x, y, valid = lane_cells()
     selfs, pairs = self_and_pairs(DOMX, DOMY)
-    reps = pairs + selfs
-    weight = np.array([2.0] * len(pairs) + [1.0] * len(selfs))
+    reps = selfs + pairs
+    weight = np.array([1.0] * SELFS + [2.0] * PAIRS)
     kap = np.array([a for a, b in reps])
     lam = np.array([b for a, b in reps])
     source = np.arange(N)
@@ -88,8 +94,9 @@
     left = np.zeros((2, REPS, N))
     left[0, : len(reps)] = np.cos(angle)
     left[1, : len(reps)] = np.where(steps % 8 == 0, 0.0, -np.sin(angle))
+    kept = np.r_[0 : len(reps), REPS + SELFS : REPS + len(reps)]
     left = left.reshape(2 * REPS, N)
-    out["left"], out["left_back"] = left, left.T
+    out["left"], out["left_back"] = left, left[kept].T
 
     phase = turn * ((kap[:, None] * x[None, :] + lam[:, None] * y[None, :]) % G)
     lane = np.arange(LANES)
@@ -117,6 +124,7 @@
         axis=1,
     )
     out["right"] = right * valid[:, None]
+    out["right_back"] = out["right"].T
 
     rate = (np.pi / (ewald_beta * G)) ** 2
     bump = np.zeros((4, REPS, HALF))
@@ -162,6 +170,10 @@
         return lax.dot_general(p, q, (dims, ((), ())), preferred_element_type=f32)
 
     return one(a[0], b[0]) + (one(a[0], b[1]) + one(a[1], b[0]))
+
+
+def dot(a, b):
+    return jnp.dot(a, b, preferred_element_type=f32)
 
 
 def splines(u):
@@ -199,8 +211,8 @@
 
 
 def body(
-    charges_any, fractions_any, bases_any, counts, basis_any, left_any, back_any, right_any, twiddle_any,
-    bump_any, along_any, out, basis, left, left_back, right, twiddle, bump, along,
+    charges_any, fractions_any, bases_any, counts, basis_any, left_any, back_any, right_any, wide_any, twiddle_any,
+    bump_any, along_any, out, basis, left, left_back, right, right_back, twiddle, bump, along,
     charges, fractions, bases, tw, bt, send_a, send_b, recv_a, recv_b,
     back_a, back_b, home_a, home_b, gt, early, sems, loads,
 ):
@@ -212,7 +224,7 @@
         for k, (source, target) in enumerate(
             (
                 (fractions_any, fractions), (bases_any, bases), (charges_any, charges), (basis_any, basis),
-                (left_any, left), (right_any, right), (twiddle_any, twiddle),
+                (left_any, left), (right_any, right), (twiddle_any, twiddle), (wide_any, right_back),
                 (bump_any, bump), (along_any, along), (back_any, left_back),
             )
         )
@@ -276,23 +288,23 @@
     for k, part in enumerate((high, low)):
         bt[k, pl.ds(MAIN, CELLS - MAIN)] = part
 
-    planes = dot3((bt[0], bt[1]), (tw[0, 0], tw[1, 0]), ((1,), (1,)))
+    planes = dot3((tw[0, 0], tw[1, 0]), (bt[0], bt[1]), ((1,), (1,)))
 
     def put(target, value, tiles):
         for t in range(tiles):
             target[:, t, :] = value[:, t * 128 : (t + 1) * 128]
 
-    def put_turned(target, value):
-        for t in range(TILES - 1):
-            target[:, t, :] = value[t * 128 : (t + 1) * 128].T
-
-    put_turned(send_a, planes[:, :N])
-    send_a[:, TILES - 1, :] = jnp.concatenate([planes[HALFTILE:, :N], planes[HALFTILE:, N:]], axis=0).T
+    put(send_a, planes[:N], TILES - 1)
+    put(send_b, planes[N:], TILES - 1)
+    send_a[:, TILES - 1, :] = jnp.concatenate([planes[:N, HALFTILE:], planes[N:, HALFTILE:]], axis=1)
     pl.semaphore_wait(barrier, N - 1)
     post(send_a, recv_a, 0)
-    put_turned(send_b, planes[:, N:])
+
+    (sz,) = spread(G, bases[2:3], (row(2, slopes),), G)
+    high, low = split(dot3((basis[0], basis[1]), split(sz)))
+    tw[0, 1] = high
+    tw[1, 1] = low
     post(send_b, recv_b, 1)
-
     for load in loading[4:]:
         load.wait()
     mine = along[pl.ds(p, 1), :]
@@ -316,14 +328,11 @@
                 jnp.where(paired, both[0] - both[1], 0.0),
             )
         )
-    (sz,) = spread(G, bases[2:3], (row(2, slopes),), G)
-    high, low = split(dot3((basis[0], basis[1]), split(sz)))
-    tw[0, 1] = high
-    tw[1, 1] = low
 
     def filtered(tiles, j):
         high, low = split(jnp.concatenate(tiles, axis=1))
-        first = dot3((left[0], left[1]), (high, low))
+        first = dot(left[...], jnp.concatenate([high, low], axis=0))
+        first = first[: 2 * REPS] + first[2 * REPS :]
         real, imag = first[:REPS], first[REPS:]
         tc, ts = twiddle[j, 0], twiddle[j, 1]
         turned = jnp.concatenate([real * tc + imag * ts, imag * tc - real * ts], axis=0)
@@ -339,10 +348,14 @@
             ],
             axis=0,
         )
-        cells = dot3(split(modes), wide, ((1,), (1,)))
+        cells = dot3(split(modes), (right_back[0], right_back[1]))
         real, imag = cells[:REPS], cells[REPS:]
-        turned = jnp.concatenate([real * tc - imag * ts, imag * tc + real * ts], axis=0)
-        return dot3((left_back[0], left_back[1]), split(turned))
+        turned = jnp.concatenate(
+            [(real * tc - imag * ts)[: SELFS + PAIRS], (imag * tc + real * ts)[SELFS : SELFS + PAIRS]],
+            axis=0,
+        )
+        both = dot(left_back[...], jnp.concatenate(split(turned), axis=0))
+        return both[:N] + both[N:]
 
     every(send_a, recv_a, 0).wait_recv()
     plane = filtered([recv_a[:, t, :] for t in range(TILES)], 0)
@@ -389,9 +402,6 @@
             sums[0] += field[cells] * wy[rows, here] * sx[x, here]
             sums[1] += field[cells] * sy[rows, here] * wx[x, here]
             sums[2] += slope[cells] * wy[rows, here] * wx[x, here]
-
-    def dot(a, b):
-        return jnp.dot(a, b, preferred_element_type=f32)
 
     def columns(j, part, here):
         rows = slice(j * N, (j + 1) * N)
@@ -430,9 +440,10 @@
 
 def solution(mesh):
     table = tables()
-    pairs = {k: np.stack(halves(table[k])) for k in ("basis", "left", "left_back", "right")}
+    pairs = {k: np.stack(halves(table[k])) for k in ("basis", "right", "right_back")}
+    pairs.update({k: side_by_side(table[k]) for k in ("left", "left_back")})
     plain = {k: table[k].astype(np.float32) for k in ("twiddle", "bump", "along")}
-    held = [pairs[k] for k in ("basis", "left", "left_back", "right")]
+    held = [pairs[k] for k in ("basis", "left", "left_back", "right", "right_back")]
     held += [plain["twiddle"], plain["bump"], plain["along"]]
     vmem = pl.BlockSpec(memory_space=pltpu.VMEM)
     smem = pl.BlockSpec(memory_space=pltpu.SMEM)
@@ -441,7 +452,7 @@
     call = pl.pallas_call(
         body,
         out_shape=jax.ShapeDtypeStruct((3, ATOM_DEV), f32),
-        in_specs=[anywhere] * 3 + [smem] + [anywhere] * 7,
+        in_specs=[anywhere] * 3 + [smem] + [anywhere] * 8,
         out_specs=vmem,
         scratch_shapes=[pltpu.VMEM(a.shape, bf16 if a.dtype != np.float32 else f32) for a in held]
         + [
@@ -455,7 +466,7 @@
             pltpu.VMEM((2, HALFTILE, G), bf16),
             pltpu.VMEM((3, 8, ATOM_DEV), f32),
             pltpu.SemaphoreType.DMA((8,)),
-            pltpu.SemaphoreType.DMA((10,)),
+            pltpu.SemaphoreType.DMA((11,)),
         ],
         compiler_params=pltpu.CompilerParams(
             collective_id=1, has_side_effects=True, vmem_limit_bytes=56 << 20

time: 39.4 us -> 37.5 us (0.952)
  Pallas kernels: 37.2 us -> 35.3 us
    pallas_call x1, Pallas kernels: 37.2 us -> 35.3 us  [local(): return call(charges.reshape(1, ATOM_DEV), fractions, bases, counts, *held)]
where the time goes in v4:
time: 37.5 us; the launch traced here: 37.3 us
  Pallas kernels  35.3 us (94%)
  local copies, waits for them, and re-layouts  1.33 us (4%)
  between operations  0.66 us (2%)
    pallas_call x1, Pallas kernels, local(): return call(charges.reshape(1, ATOM_DEV), fractions, bases, counts, *held)  35.3 us
    unnamed x1, local copies, waits for them, and re-layouts  1.33 us

profile of v4, /device:TPU:1, one launch (start us, length us, event | category | flops | bytes accessed | tf_op | source)
XLA Modules:
  0.0 37.3 jit_solution(10395222356259525130)
XLA Ops:
  0.7 35.3 %shard_map.118 = f32[3,1024]{1,0:T(4,128)} custom-call(f32[1,1024]{1,0:T(1,128)} %bitcast.1, f32[3,1024]{1,0:T(4,128)} %fractions_any.1, s32[3,1024]{1,0:T(4,128)} %bases_any.1, s32[1]{0:T(128)S(6)} %copy.14.counts, bf16[2,256,256]{2,1,0:T(8,128)(2,1)} %constant.16.clone.basis_any, bf16[288,256]{1,0:T(8,128)(2,1)} %constant.17.clone.left_any, ...), custom_call_target="tpu_custom_call" | custom-call | tf_op jit(solution)/shard_map/pallas_call | solution.py:477
  35.9 1.3 %copy.15 = f32[3,1024]{1,0:T(4,128)} copy(f32[3,1024]{1,0:T(4,128)} %shard_map.118) | data formatting | bytes 24576

commit v5 on v4

--- a/solution.py
+++ b/solution.py
@@ -33,7 +33,7 @@
 
 def side_by_side(table):
     high, low = halves(table)
-    return np.block([[high, high], [low, np.zeros_like(low)]])
+    return np.concatenate([high, low, high], axis=1)
 
 
 def halves(table):
@@ -165,11 +165,10 @@
     return high, (value - high.astype(f32)).astype(bf16)
 
 
-def dot3(a, b, dims=((1,), (0,))):
-    def one(p, q):
-        return lax.dot_general(p, q, (dims, ((), ())), preferred_element_type=f32)
-
-    return one(a[0], b[0]) + (one(a[0], b[1]) + one(a[1], b[0]))
+def dot3(a, b, across=0):
+    left = jnp.concatenate([a[0], a[1], a[0]], axis=1)
+    right = jnp.concatenate([b[0], b[0], b[1]], axis=across)
+    return lax.dot_general(left, right, (((1,), (across,)), ((), ())), preferred_element_type=f32)
 
 
 def dot(a, b):
@@ -245,18 +244,21 @@
     def post(source, target, which):
         for where in peers:
             pltpu.make_async_remote_copy(
-                src_ref=source.at[where[0] * 4 + where[1]], dst_ref=target.at[p],
+                src_ref=source.at[pl.ds(where[0] * 4 + where[1], 1)], dst_ref=target.at[pl.ds(p, 1)],
                 send_sem=sems.at[2 * which], recv_sem=sems.at[2 * which + 1],
                 device_id=where, device_id_type=MESH,
             ).start()
-        target[pl.ds(p, 1)] = source[pl.ds(p, 1)]
-
-    def every(source, target, which):
-        return pltpu.make_async_remote_copy(
-            src_ref=source.at[pl.ds(0, N - 1)], dst_ref=target.at[pl.ds(0, N - 1)],
-            send_sem=sems.at[2 * which], recv_sem=sems.at[2 * which + 1],
-            device_id=peers[0], device_id_type=MESH,
-        )
+        pltpu.make_async_copy(
+            source.at[pl.ds(p, 1)], target.at[pl.ds(p, 1)], sems.at[2 * which + 1]
+        ).start()
+
+    def arrived(target, which):
+        pltpu.make_async_copy(target, target, sems.at[2 * which + 1]).wait()
+
+    def sent(source, which):
+        for first, rows in [(0, N - 8)] + [(k, 1) for k in range(N - 8, N - 1)]:
+            part = source.at[pl.ds(first, rows)]
+            pltpu.make_async_copy(part, part, sems.at[2 * which]).wait()
 
     for load in loading[:3]:
         load.wait()
@@ -288,15 +290,11 @@
     for k, part in enumerate((high, low)):
         bt[k, pl.ds(MAIN, CELLS - MAIN)] = part
 
-    planes = dot3((tw[0, 0], tw[1, 0]), (bt[0], bt[1]), ((1,), (1,)))
-
-    def put(target, value, tiles):
-        for t in range(tiles):
-            target[:, t, :] = value[:, t * 128 : (t + 1) * 128]
-
-    put(send_a, planes[:N], TILES - 1)
-    put(send_b, planes[N:], TILES - 1)
-    send_a[:, TILES - 1, :] = jnp.concatenate([planes[:N, HALFTILE:], planes[N:, HALFTILE:]], axis=1)
+    planes = dot3((tw[0, 0], tw[1, 0]), (bt[0], bt[1]), 1)
+
+    send_a[:, :HALFTILE] = planes[:N, :HALFTILE]
+    send_b[...] = planes[N:, :HALFTILE]
+    send_a[:, HALFTILE:] = jnp.concatenate([planes[:N, HALFTILE:], planes[N:, HALFTILE:]], axis=1)
     pl.semaphore_wait(barrier, N - 1)
     post(send_a, recv_a, 0)
 
@@ -329,10 +327,9 @@
             )
         )
 
-    def filtered(tiles, j):
-        high, low = split(jnp.concatenate(tiles, axis=1))
-        first = dot(left[...], jnp.concatenate([high, low], axis=0))
-        first = first[: 2 * REPS] + first[2 * REPS :]
+    def filtered(arrival, j):
+        high, low = split(arrival)
+        first = dot(left[...], jnp.concatenate([high, high, low], axis=0))
         real, imag = first[:REPS], first[REPS:]
         tc, ts = twiddle[j, 0], twiddle[j, 1]
         turned = jnp.concatenate([real * tc + imag * ts, imag * tc - real * ts], axis=0)
@@ -354,22 +351,22 @@
             [(real * tc - imag * ts)[: SELFS + PAIRS], (imag * tc + real * ts)[SELFS : SELFS + PAIRS]],
             axis=0,
         )
-        both = dot(left_back[...], jnp.concatenate(split(turned), axis=0))
-        return both[:N] + both[N:]
-
-    every(send_a, recv_a, 0).wait_recv()
-    plane = filtered([recv_a[:, t, :] for t in range(TILES)], 0)
-    put(back_a, plane, TILES - 1)
-    back_b[:, TILES - 1, :] = plane[:, HALFTILE:]
+        high, low = split(turned)
+        return dot(left_back[...], jnp.concatenate([high, high, low], axis=0))
+
+    arrived(recv_a, 0)
+    plane = filtered(recv_a[...], 0)
+    back_a[...] = plane[:, :HALFTILE]
+    back_b[:, HALFTILE:] = plane[:, HALFTILE:]
     post(back_a, home_a, 2)
-    every(send_b, recv_b, 1).wait_recv()
-    plane = filtered([recv_b[:, t, :] for t in range(TILES - 1)] + [recv_a[:, TILES - 1, :]], 1)
-    put(back_b, plane, TILES - 1)
-    back_b[:, TILES - 1, :] += plane[:, HALFTILE:]
+    arrived(recv_b, 1)
+    plane = filtered(jnp.concatenate([recv_b[...], recv_a[:, HALFTILE:]], axis=1), 1)
+    back_b[:, :HALFTILE] = plane[:, :HALFTILE]
+    back_b[:, HALFTILE:] += plane[:, HALFTILE:]
     post(back_b, home_b, 3)
 
-    every(send_a, recv_a, 0).wait_send()
-    every(send_b, recv_b, 1).wait_send()
+    sent(send_a, 0)
+    sent(send_b, 1)
     chunk = 256
 
     def fold(part):
@@ -403,39 +400,44 @@
             sums[1] += field[cells] * sy[rows, here] * wx[x, here]
             sums[2] += slope[cells] * wy[rows, here] * wx[x, here]
 
-    def columns(j, part, here):
+    def fields(j, part, here):
         rows = slice(j * N, (j + 1) * N)
         high = tw[0, part, rows, here]
-        return jnp.concatenate([high, high], axis=0), tw[1, part, rows, here]
-
-    def fields(j, part, here):
-        twice, low = columns(j, part, here)
-        return dot(gt[j, :HALFTILE], twice) + dot(gt[j, :HALFTILE, :N], low)
+        parts = [high, high, tw[1, part, rows, here]]
+        if j == 0:
+            return dot(gt[0, :HALFTILE, : 3 * N], jnp.concatenate(parts, axis=0))
+        other = tw[0, part, :N, here]
+        whole = dot(gt[1], jnp.concatenate(parts + [other], axis=0))
+        rest = dot(gt[0, HALFTILE:, : 2 * N], jnp.concatenate([other, tw[1, part, :N, here]], axis=0))
+        return whole[:HALFTILE], whole[HALFTILE:] + rest
 
     def turn(home, j):
         for t in range(TILES - 1):
             rows = pl.ds(t * 128, 128)
-            gt[j, rows, :N], gt[j, rows, N:] = split(home[:, t, :].T)
+            high, low = split(home[:, t * 128 : (t + 1) * 128].T)
+            gt[j, rows] = jnp.concatenate([high, low, high, jnp.zeros_like(high)], axis=1)
 
     chunks = [slice(r, r + chunk) for r in range(0, ATOM_DEV, chunk)]
-    every(back_a, home_a, 2).wait_recv()
+    arrived(home_a, 2)
     turn(home_a, 0)
     for here in chunks:
         for a, part in enumerate(gather(here, fields(0, 0, here), fields(0, 1, here))):
             early[a, :, here] = part
-    every(back_b, home_b, 3).wait_recv()
+    arrived(home_b, 3)
     turn(home_b, 1)
-    shared = home_b[:, TILES - 1, :].T
-    shared = split(jnp.concatenate([shared[:64], shared[64:]], axis=1))
+    shared = home_b[:, HALFTILE:].T
+    (high, other), (low, least) = ((part[64:], part[:64]) for part in split(shared))
+    gt[1, HALFTILE:] = jnp.concatenate([high, low, high, other], axis=1)
+    gt[0, HALFTILE:, : 2 * N] = jnp.concatenate([least, other], axis=1)
     for here in chunks:
-        sums = gather(here, fields(1, 0, here), fields(1, 1, here))
-        tails = [dot3(shared, (tw[0, k, :, here], tw[1, k, :, here])) for k in range(2)]
-        gather_tail(sums, here, *tails)
+        (field, field_tail), (slope, slope_tail) = fields(1, 0, here), fields(1, 1, here)
+        sums = gather(here, field, slope)
+        gather_tail(sums, here, field_tail, slope_tail)
         for a in range(3):
             total = jnp.sum(sums[a] + early[a, :, here], axis=0, keepdims=True)
             out[a : a + 1, here] = -weighted[:, here] * total
-    every(back_a, home_a, 2).wait_send()
-    every(back_b, home_b, 3).wait_send()
+    sent(back_a, 2)
+    sent(back_b, 3)
 
 
 def solution(mesh):
@@ -448,10 +450,10 @@
     vmem = pl.BlockSpec(memory_space=pltpu.VMEM)
     smem = pl.BlockSpec(memory_space=pltpu.SMEM)
     anywhere = pl.BlockSpec(memory_space=pl.ANY)
-    five, six = (pltpu.VMEM((N, rows, 128), f32) for rows in (TILES - 1, TILES))
+    five, six = (pltpu.VMEM((N, lanes), f32) for lanes in (HALFTILE, LANES))
     call = pl.pallas_call(
         body,
-        out_shape=jax.ShapeDtypeStruct((3, ATOM_DEV), f32),
+        out_shape=pltpu.VMEM((3, ATOM_DEV), f32),
         in_specs=[anywhere] * 3 + [smem] + [anywhere] * 8,
         out_specs=vmem,
         scratch_shapes=[pltpu.VMEM(a.shape, bf16 if a.dtype != np.float32 else f32) for a in held]
@@ -463,7 +465,7 @@
             pltpu.VMEM((2, CELLS, ATOM_DEV), bf16),
             six, five, six, five,
             five, six, five, six,
-            pltpu.VMEM((2, HALFTILE, G), bf16),
+            pltpu.VMEM((2, CELLS, 4 * N), bf16),
             pltpu.VMEM((3, 8, ATOM_DEV), f32),
             pltpu.SemaphoreType.DMA((8,)),
             pltpu.SemaphoreType.DMA((11,)),

time: 37.5 us -> 35.5 us (0.947)
  Pallas kernels: 35.3 us -> 34.1 us
  local copies, waits for them, and re-layouts: 1.33 us -> 0.61 us
    pallas_call x1, Pallas kernels: 35.3 us -> 34.1 us  [local(): return call(charges.reshape(1, ATOM_DEV), fractions, bases, counts, *held)]
    unnamed x1, local copies, waits for them, and re-layouts: 1.33 us -> 0.61 us
where the time goes in v5:
time: 35.5 us; the launch traced here: 35.4 us
  Pallas kernels  34.1 us (96%)
  between operations  0.66 us (2%)
  local copies, waits for them, and re-layouts  0.61 us (2%)
    pallas_call x1, Pallas kernels, local(): return call(charges.reshape(1, ATOM_DEV), fractions, bases, counts, *held)  34.1 us

profile of v5, /device:TPU:1, one launch (start us, length us, event | category | flops | bytes accessed | tf_op | source)
XLA Modules:
  0.0 35.4 jit_solution(16978331674434177926)
XLA Ops:
  0.7 34.1 %shard_map.118 = f32[3,1024]{1,0:T(4,128)S(1)} custom-call(f32[1,1024]{1,0:T(1,128)} %bitcast.1, f32[3,1024]{1,0:T(4,128)} %fractions_any.1, s32[3,1024]{1,0:T(4,128)} %bases_any.1, s32[1]{0:T(128)S(6)} %copy.15.counts, bf16[2,256,256]{2,1,0:T(8,128)(2,1)} %constant.16.clone.basis_any, bf16[144,384]{1,0:T(8,128)(2,1)} %constant.17.clone.left_any, ...), custom_call_target="tpu_custom_call" | custom-call | tf_op jit(solution)/shard_map/pallas_call | solution.py:479
  34.7 0.6 %copy.14 = f32[3,1024]{1,0:T(4,128)} copy(f32[3,1024]{1,0:T(4,128)S(1)} %shard_map.118) | data formatting | bytes 24576

commit v6 on v5

--- a/solution.py
+++ b/solution.py
@@ -154,10 +154,24 @@
 
 def far_first():
     hops = (0, 1, 2, 1)
-    offsets = [(y, x, c, z) for y in range(4) for x in range(4) for c in range(2) for z in range(4)]
-    spread_out = np.random.RandomState(1).permutation(len(offsets))
-    offsets = [offsets[k] for k in spread_out if any(offsets[k])]
-    return sorted(offsets, key=lambda o: -(hops[o[0]] + hops[o[1]] + hops[o[3]]))
+    links = {0: (0, 0), 1: (2, 0), 2: (1, 1), 3: (0, 2)}
+    left = [(y, x, c, z) for y in range(4) for x in range(4) for c in range(2) for z in range(4)]
+    left = [o for o in left if any(o)]
+    used, order = np.zeros(6), []
+    while left:
+        far = max(hops[o[0]] + hops[o[1]] + hops[o[3]] for o in left)
+        best = None
+        for o in left:
+            if hops[o[0]] + hops[o[1]] + hops[o[3]] < far:
+                continue
+            load = used + np.array(links[o[0]] + links[o[1]] + links[o[3]])
+            key = (load.max(), (load**2).sum())
+            if best is None or key < best[0]:
+                best = (key, o, load)
+        order.append(best[1])
+        left.remove(best[1])
+        used = best[2]
+    return order
 
 
 def split(value):

time: 35.5 us -> 35 us (0.986)
  Pallas kernels: 34.1 us -> 33.6 us
    pallas_call x1, Pallas kernels: 34.1 us -> 33.6 us  [local(): return call(charges.reshape(1, ATOM_DEV), fractions, bases, counts, *held)]
where the time goes in v6:
time: 35 us; the launch traced here: 34.8 us
  Pallas kernels  33.6 us (96%)
  between operations  0.66 us (2%)
  local copies, waits for them, and re-layouts  0.61 us (2%)
    pallas_call x1, Pallas kernels, local(): return call(charges.reshape(1, ATOM_DEV), fractions, bases, counts, *held)  33.6 us

profile of v6, /device:TPU:1, one launch (start us, length us, event | category | flops | bytes accessed | tf_op | source)
XLA Modules:
  0.0 34.8 jit_solution(17180519161384704142)
XLA Ops:
  0.7 33.6 %shard_map.118 = f32[3,1024]{1,0:T(4,128)S(1)} custom-call(f32[1,1024]{1,0:T(1,128)} %bitcast.1, f32[3,1024]{1,0:T(4,128)} %fractions_any.1, s32[3,1024]{1,0:T(4,128)} %bases_any.1, s32[1]{0:T(128)S(6)} %copy.15.counts, bf16[2,256,256]{2,1,0:T(8,128)(2,1)} %constant.16.clone.basis_any, bf16[144,384]{1,0:T(8,128)(2,1)} %constant.17.clone.left_any, ...), custom_call_target="tpu_custom_call" | custom-call | tf_op jit(solution)/shard_map/pallas_call | solution.py:493
  34.2 0.6 %copy.14 = f32[3,1024]{1,0:T(4,128)} copy(f32[3,1024]{1,0:T(4,128)S(1)} %shard_map.118) | data formatting | bytes 24576

commit v7 on v6

--- a/solution.py
+++ b/solution.py
@@ -304,19 +304,25 @@
     for k, part in enumerate((high, low)):
         bt[k, pl.ds(MAIN, CELLS - MAIN)] = part
 
-    planes = dot3((tw[0, 0], tw[1, 0]), (bt[0], bt[1]), 1)
-
-    send_a[:, :HALFTILE] = planes[:N, :HALFTILE]
-    send_b[...] = planes[N:, :HALFTILE]
-    send_a[:, HALFTILE:] = jnp.concatenate([planes[:N, HALFTILE:], planes[N:, HALFTILE:]], axis=1)
+    def planes(rows, first, last):
+        cells = slice(first, last)
+        return dot3((tw[0, 0, rows], tw[1, 0, rows]), (bt[0, cells], bt[1, cells]), 1)
+
+    plane = planes(slice(0, N), 0, CELLS)
+    send_a[:, :HALFTILE] = plane[:, :HALFTILE]
+    send_a[:, HALFTILE:] = jnp.concatenate(
+        [plane[:, HALFTILE:], planes(slice(N, G), HALFTILE, CELLS)], axis=1
+    )
     pl.semaphore_wait(barrier, N - 1)
     post(send_a, recv_a, 0)
+
+    send_b[...] = planes(slice(N, G), 0, HALFTILE)
+    post(send_b, recv_b, 1)
 
     (sz,) = spread(G, bases[2:3], (row(2, slopes),), G)
     high, low = split(dot3((basis[0], basis[1]), split(sz)))
     tw[0, 1] = high
     tw[1, 1] = low
-    post(send_b, recv_b, 1)
     for load in loading[4:]:
         load.wait()
     mine = along[pl.ds(p, 1), :]

time: 35 us -> 34.9 us (level)
  no operation moved by 1% of the time
where the time goes in v7:
time: 34.9 us; the launch traced here: 34.8 us
  Pallas kernels  33.6 us (96%)
  between operations  0.66 us (2%)
  local copies, waits for them, and re-layouts  0.61 us (2%)
    pallas_call x1, Pallas kernels, local(): return call(charges.reshape(1, ATOM_DEV), fractions, bases, counts, *held)  33.6 us

profile of v7, /device:TPU:1, one launch (start us, length us, event | category | flops | bytes accessed | tf_op | source)
XLA Modules:
  0.0 34.8 jit_solution(13393051406284557551)
XLA Ops:
  0.7 33.6 %shard_map.118 = f32[3,1024]{1,0:T(4,128)S(1)} custom-call(f32[1,1024]{1,0:T(1,128)} %bitcast.1, f32[3,1024]{1,0:T(4,128)} %fractions_any.1, s32[3,1024]{1,0:T(4,128)} %bases_any.1, s32[1]{0:T(128)S(6)} %copy.15.counts, bf16[2,256,256]{2,1,0:T(8,128)(2,1)} %constant.16.clone.basis_any, bf16[144,384]{1,0:T(8,128)(2,1)} %constant.17.clone.left_any, ...), custom_call_target="tpu_custom_call" | custom-call | tf_op jit(solution)/shard_map/pallas_call | solution.py:499
  34.2 0.6 %copy.14 = f32[3,1024]{1,0:T(4,128)} copy(f32[3,1024]{1,0:T(4,128)S(1)} %shard_map.118) | data formatting | bytes 24576
